TPU v7x, 128 devices: a whole 4x4x4 slice. The times are simulated.
128 devices in a mesh: lat: 2 (over x_lo), lon: 64 (over x_hi, z, y, core).
Axes of the slice: x: 4 (x_hi: 2, x_lo: 2; x = x_hi * 2 + x_lo), y: 4, z: 4, core: 2. Of those that a mesh axis runs over, the one named last changes fastest.
Arguments:
- fields: bfloat16 [16, 4096, 512], P('lat', 'lon'), may hold values from -6 to 6
- surface: int32 [16, 4096], P('lat', 'lon'), may hold values from 0 to 2
- surface_table: float32 [3, 512], replicated, may hold values from -4 to 4
- logit_scale: float32 [8], replicated, may hold values from 2 to 12
- w_qkv: bfloat16 [512, 1536], replicated, may hold values from -0.25 to 0.25
- w_out: bfloat16 [512, 512], replicated, may hold values from -0.25 to 0.25
- w_merge: bfloat16 [2048, 1024], P(('lat', 'lon')), may hold values from -0.125 to 0.125
- w_split: bfloat16 [1024, 2048], P(('lat', 'lon')), may hold values from -0.1875 to 0.1875
- cotangent: bfloat16 [16, 4096, 512], P('lat', 'lon'), may hold values from -6 to 6
Outputs:
- decoded: bfloat16 [16, 4096, 512], P('lat', 'lon')
- grad_fields: bfloat16 [16, 4096, 512], P('lat', 'lon')
- grad_qkv_weight: float32 [512, 1536], P(('lat', 'lon'))
- grad_out_weight: float32 [512, 512], P(('lat', 'lon'))
- grad_merge_weight: float32 [2048, 1024], P(('lat', 'lon'))
- grad_split_weight: float32 [1024, 2048], P(('lat', 'lon'))
All inputs are finite; a program needn't handle non-finite values.
Results may differ from a plain program's by a relative error of at most 0.017.
Values may be sent and summed in bfloat16 or wider, within the bound.
No kernel may reach another device: no remote copies, remote signals or barrier semaphores. Data moves between devices by JAX's collectives and lax.ppermute only.
A program may use at most 128 MiB of HBM per device.

v0:
```python
import jax
import jax.numpy as jnp
from jax import lax
from jax.sharding import PartitionSpec as P

HEADS = 8
WIN = 8
SHIFT = 4


EPS_NORM = 1e-05
EPS_UNIT = 1e-06


def from_behind(value, axis, steps):
    count = lax.axis_size(axis)
    pairs = [(source, (source + steps) % count) for source in range(count)]
    return lax.ppermute(value, axis, pairs)


def layer_norm(values):
    centre = values - jnp.mean(values, axis=-1, keepdims=True)
    spread = jnp.mean(centre * centre, axis=-1, keepdims=True)
    return centre * lax.rsqrt(spread + EPS_NORM)


def rounded_norm(values):
    return layer_norm(values).astype(jnp.bfloat16)


def inner(left, right):
    return lax.dot_general(
        left, right, (((0,), (0,)), ((), ())), preferred_element_type=jnp.float32
    )


def merge_cells(grid):
    lat_rows, lon_cols, feat_count = grid.shape
    blocks = grid.reshape(lat_rows // 2, 2, lon_cols // 2, 2, feat_count).transpose(0, 2, 1, 3, 4)
    return blocks.reshape(lat_rows * lon_cols // 4, 4 * feat_count)


def split_cells(flat, lat_rows, lon_cols):
    feat_count = flat.shape[1] // 4
    blocks = flat.reshape(lat_rows // 2, lon_cols // 2, 2, 2, feat_count).transpose(0, 2, 1, 3, 4)
    return blocks.reshape(lat_rows, lon_cols, feat_count)


def window_attention(packed, region, logit_scale):
    grid_rows, grid_cols, triple_width = packed.shape
    model_width = triple_width // 3
    head_size = model_width // HEADS
    win_rows = grid_rows // WIN
    win_cols = grid_cols // WIN
    windows = packed.reshape(win_rows, WIN, win_cols, WIN, 3, HEADS, head_size)
    windows = windows.transpose(0, 2, 1, 3, 4, 5, 6).reshape(
        win_rows * win_cols, WIN * WIN, 3, HEADS, head_size
    )
    queries = windows[:, :, 0]
    key_rows = windows[:, :, 1]
    values = windows[:, :, 2].astype(jnp.bfloat16)
    query_unit = (
        queries * lax.rsqrt(jnp.sum(queries * queries, axis=-1, keepdims=True) + EPS_UNIT)
    ).astype(jnp.bfloat16)
    key_unit = (
        key_rows * lax.rsqrt(jnp.sum(key_rows * key_rows, axis=-1, keepdims=True) + EPS_UNIT)
    ).astype(jnp.bfloat16)
    scores = jnp.einsum("wqhd,wkhd->whqk", query_unit, key_unit, preferred_element_type=jnp.float32)
    scores = scores * logit_scale[None, :, None, None]
    labels = jnp.broadcast_to(region.reshape(win_rows, 1, WIN, 1), (win_rows, win_cols, WIN, WIN))
    labels = labels.reshape(win_rows * win_cols, WIN * WIN)
    same_region = labels[:, :, None] == labels[:, None, :]
    exponent = jnp.where(same_region[:, None], jnp.exp(scores), jnp.float32(0.0))
    weights = (exponent / jnp.sum(exponent, axis=-1, keepdims=True)).astype(jnp.bfloat16)
    attended = jnp.einsum(
        "whqk,wkhd->wqhd", weights, values, preferred_element_type=jnp.float32
    ).astype(jnp.bfloat16)
    attended = attended.reshape(win_rows, win_cols, WIN, WIN, model_width).transpose(0, 2, 1, 3, 4)
    return attended.reshape(grid_rows, grid_cols, model_width)


def fetch_rim(field):
    top_strip = from_behind(field[:SHIFT], "lat", -1)
    side_strip = from_behind(field[:, :SHIFT], "lon", -1)
    corner = from_behind(side_strip[:SHIFT], "lat", -1)
    upper = jnp.concatenate([field[SHIFT:, SHIFT:], side_strip[SHIFT:]], axis=1)
    lower = jnp.concatenate([top_strip[:, SHIFT:], corner], axis=1)
    return jnp.concatenate([upper, lower], axis=0)


def return_rim(shifted):
    side_back = from_behind(shifted[:, -SHIFT:], "lon", 1)
    top_back = from_behind(shifted[-SHIFT:, :-SHIFT], "lat", 1)
    corner = from_behind(side_back[-SHIFT:], "lat", 1)
    upper = jnp.concatenate([corner, top_back], axis=1)
    lower = jnp.concatenate([side_back[:-SHIFT], shifted[:-SHIFT, :-SHIFT]], axis=1)
    return jnp.concatenate([upper, lower], axis=0)


def per_device(
    fields, surface, surface_table, logit_scale, w_qkv, w_out, w_merge, w_split, cotangent
):
    lat_rows, lon_cols, model_width = fields.shape
    token_count = lat_rows * lon_cols
    split_full = lax.all_gather(w_split, ("lat", "lon"), axis=0, tiled=True)
    merge_full = lax.all_gather(w_merge, ("lat", "lon"), axis=0, tiled=True)
    classes = (surface[:, :, None] == jnp.arange(3, dtype=jnp.int32)).astype(jnp.float32)
    table_rows = jnp.dot(classes.reshape(-1, 3), surface_table, precision=lax.Precision.HIGHEST)
    embedded = fields.astype(jnp.float32) + table_rows.reshape(lat_rows, lon_cols, model_width)
    normed, normed_back = jax.vjp(rounded_norm, embedded)
    shifted = fetch_rim(normed)
    flat_shifted = shifted.reshape(token_count, model_width)
    packed = jnp.dot(flat_shifted, w_qkv, preferred_element_type=jnp.float32).reshape(
        lat_rows, lon_cols, 3 * model_width
    )
    row_index = lax.axis_index("lat") * lat_rows + jnp.arange(lat_rows, dtype=jnp.int32)
    region = (row_index >= lat_rows * lax.axis_size("lat") - SHIFT).astype(jnp.int32)
    attended, attend_back = jax.vjp(
        lambda packed_qkv: window_attention(packed_qkv, region, logit_scale), packed
    )
    flat_att = attended.reshape(token_count, model_width)
    projected = jnp.dot(flat_att, w_out, preferred_element_type=jnp.float32).astype(jnp.bfloat16)
    projected = projected.reshape(lat_rows, lon_cols, model_width)
    skip = (embedded + return_rim(projected).astype(jnp.float32)).astype(jnp.bfloat16)
    merged = merge_cells(skip)
    merged_norm, norm_back = jax.vjp(rounded_norm, merged.astype(jnp.float32))
    coarse_pre = jnp.dot(merged_norm, merge_full, preferred_element_type=jnp.float32)
    coarse_full, gelu_back = jax.vjp(jax.nn.gelu, coarse_pre)
    coarse = coarse_full.astype(jnp.bfloat16)
    split_out = jnp.dot(coarse, split_full, preferred_element_type=jnp.float32)
    decoded = (skip.astype(jnp.float32) + split_cells(split_out, lat_rows, lon_cols)).astype(
        jnp.bfloat16
    )
    merged_cot = merge_cells(cotangent)
    grad_coarse = jnp.dot(merged_cot, split_full.T, preferred_element_type=jnp.float32)
    grad_pre = gelu_back(grad_coarse)[0].astype(jnp.bfloat16)
    grad_mnorm = jnp.dot(grad_pre, merge_full.T, preferred_element_type=jnp.float32).astype(
        jnp.bfloat16
    )
    grad_skip = cotangent.astype(jnp.float32) + split_cells(
        norm_back(grad_mnorm)[0], lat_rows, lon_cols
    )
    grad_shifted = fetch_rim(grad_skip.astype(jnp.bfloat16))
    flat_grad = grad_shifted.reshape(token_count, model_width)
    grad_att = jnp.dot(flat_grad, w_out.T, preferred_element_type=jnp.float32).astype(jnp.bfloat16)
    grad_packed = attend_back(grad_att.reshape(lat_rows, lon_cols, model_width))[0]
    grad_packed = grad_packed.reshape(token_count, 3 * model_width).astype(jnp.bfloat16)
    grad_split = lax.psum_scatter(
        inner(coarse, merged_cot), ("lat", "lon"), scatter_dimension=0, tiled=True
    )
    grad_merge = lax.psum_scatter(
        inner(merged_norm, grad_pre), ("lat", "lon"), scatter_dimension=0, tiled=True
    )
    qkv_part = inner(flat_shifted, grad_packed)
    out_part = inner(flat_att, flat_grad)
    fine_grads = lax.psum_scatter(
        jnp.concatenate([qkv_part, out_part], axis=1),
        ("lat", "lon"),
        scatter_dimension=0,
        tiled=True,
    )
    grad_qkv_weight = fine_grads[:, : 3 * model_width]
    grad_out_weight = fine_grads[:, 3 * model_width :]
    grad_normed = jnp.dot(grad_packed, w_qkv.T, preferred_element_type=jnp.float32).astype(
        jnp.bfloat16
    )
    grad_normed = return_rim(grad_normed.reshape(lat_rows, lon_cols, model_width))
    grad_fields = (grad_skip + normed_back(grad_normed)[0]).astype(jnp.bfloat16)
    return (decoded, grad_fields, grad_qkv_weight, grad_out_weight, grad_merge, grad_split)


def solution(mesh):
    in_specs = (
        P("lat", "lon", None),
        P("lat", "lon"),
        P(),
        P(),
        P(),
        P(),
        P(("lat", "lon"), None),
        P(("lat", "lon"), None),
        P("lat", "lon", None),
    )
    out_specs = (
        P("lat", "lon", None),
        P("lat", "lon", None),
        P(("lat", "lon"), None),
        P(("lat", "lon"), None),
        P(("lat", "lon"), None),
        P(("lat", "lon"), None),
    )
    return jax.shard_map(
        per_device, mesh=mesh, in_specs=in_specs, out_specs=out_specs, check_vma=False
    )
```

profile of v0, /device:TPU:1, one launch (start us, length us, event | category | flops | bytes accessed | tf_op | source)
XLA Modules:
  0.0 1945.8 jit_solution(8064621526363143319)
XLA Ops:
  8.7 1.8 fusion.57
  11.1 1.5 collective-permute-start
  13.3 1.3 collective-permute-start.1
  15.4 1.3 collective-permute-start.2
  16.9 1.7 copy.52
  20.7 1.8 convolution_bitcast_fusion
  22.5 1.4 copy.53
  23.9 2.6 copy-done.6
  26.7 1.5 copy.86
  28.2 4.7 fusion.50
  32.9 2.9 copy.88
  35.8 2.9 copy.87
  38.7 2.1 fusion.11
  40.8 1.9 fusion.13
  43.7 1.3 copy-done.10
  45.1 1.6 fusion.16
  46.7 1.7 copy.60
  48.4 1.4 reshape.212
  52.3 5.0 collective-permute-start.3
  59.3 3.6 collective-permute-done.3
  65.7 1.3 collective-permute-done.4
  67.1 2.2 fusion.30
  69.3 1.8 reshape.227
  72.1 1.4 copy.62
  73.5 2.1 reshape.225
  75.6 1.6 bitcast_reduce_fusion
  77.3 2.2 multiply_reduce_fusion.1
  80.1 130.7 %all-gather.5.cloned.1.call-done = bf16[1024,2048]{1,0:T(8,128)(2,1)} async-done(((bf16[8,2048]{1,0:T(8,128)(2,1)}), bf16[1024,2048]{1,0:T(8,128)(2,1)}) %all-gather.5.cloned.1.call-update) | async-done | bytes 4194320 | tf_op jit(solution)/shard_map/all_gather | solution.py:105
  210.8 4.7 fusion.58
  215.5 193.4 %all-gather.3.cloned.1.call-done = bf16[2048,1024]{1,0:T(8,128)(2,1)} async-done(((bf16[16,1024]{1,0:T(8,128)(2,1)}), bf16[2048,1024]{1,0:T(8,128)(2,1)}) %all-gather.3.cloned.1.call-update) | async-done | bytes 4194320 | tf_op jit(solution)/shard_map/all_gather | solution.py:106
  408.9 4.3 fusion.29
  413.2 1.6 multiply_reduce_fusion
  416.3 3.1 reshape.219
  419.4 2.6 copy.93
  422.0 2.9 reshape.220
  424.9 1.4 fusion.22
  428.3 1.4 collective-permute-done.6
  431.5 1.7 collective-permute-done.7
  434.0 1.5 reshape.222
  435.5 2.4 copy.67
  437.9 3.3 fusion.6
  441.4 2.9 fusion.9
  446.7 1.5 fusion.60
  449.4 2.6 add_convert_fusion
  452.0 4.9 copy.73
  456.9 4.3 copy.74
  461.1 5.4 convert_element_type.189
  466.5 2.5 fusion.59
  469.0 2.3 pad_maximum_fusion
  472.0 4.6 fusion.45
  477.8 4.5 fusion.43
  482.4 3.0 fusion.44
  485.4 1.9 reshape.215
  487.3 2.7 copy.94
  490.0 2.9 reshape.216
  492.9 2.6 convolution_convert_fusion.6
  495.6 3.9 collective-permute-start.9
  502.3 7.3 collective-permute-done.10
  510.7 1.3 add_convert_fusion.1
  512.1 116.5 %all-reduce.6.cloned.1.call-done = f32[512,2048]{1,0:T(8,128)} async-done(((f32[512,2048]{1,0:T(8,128)}), f32[512,2048]{1,0:T(8,128)}) %all-reduce.6.cloned.1.call-update) | async-done | bytes 4194320
  628.6 1.4 dynamic-slice.2
  630.0 1.4 constant_dynamic-slice_fusion
  631.4 641.7 %reduce-scatter.3.cloned.1.call-done = f32[16,1024]{1,0:T(8,128)} async-done(((f32[2048,1024]{1,0:T(8,128)}), f32[16,1024]{1,0:T(8,128)}) %reduce-scatter.3.cloned.1.call-update) | async-done | bytes 65552 | tf_op jit(solution)/shard_map/reduce_scatter | solution.py:151
  1273.1 665.8 %reduce-scatter.5.cloned.1.call-done = f32[8,2048]{1,0:T(8,128)} async-done(((f32[1024,2048]{1,0:T(8,128)}), f32[8,2048]{1,0:T(8,128)}) %reduce-scatter.5.cloned.1.call-update) | async-done | bytes 65552 | tf_op jit(solution)/shard_map/reduce_scatter | solution.py:148
  (160 shorter events, 31.1 us)
Async XLA Ops:
  7.2 44.6 %copy-start = (bf16[512,512]{1,0:T(8,128)(2,1)S(1)}, bf16[512,512]{1,0:T(8,128)(2,1)}, u32[]{:S(2)}) copy-start(bf16[512,512]{1,0:T(8,128)(2,1)} %param.14) | copy-start | bytes 1572868
  7.2 203.6 %all-gather.5.cloned.1.call-start = ((), (), s32[]{:S(2)}) async-start(), calls=%async_computation.3 | async-start | bytes 4227072 | tf_op jit(solution)/shard_map/all_gather | solution.py:105
  7.9 401.0 %all-gather.3.cloned.1.call-start = ((), (), s32[]{:S(2)}) async-start(), calls=%async_computation.2 | async-start | bytes 4227072 | tf_op jit(solution)/shard_map/all_gather | solution.py:106
  8.7 620.0 %all-reduce.6.cloned.1.call-start = ((), (), s32[]{:S(2)}) async-start(), calls=%async_computation.6 | async-start | bytes 8388608
  11.1 4.4 collective-permute-start
  13.3 5.5 collective-permute-start.1
  15.4 4.4 collective-permute-start.2
  19.9 0.8 copy-start.24
  23.9 2.6 copy-start.6
  38.7 4.1 copy-start.2
  38.7 4.1 copy-start.4
  38.7 4.1 copy-start.36
  42.7 1.0 copy-start.26
  42.8 1.0 copy-start.28
  42.8 2.3 copy-start.20
  43.7 1.4 copy-start.10
  43.7 1.4 copy-start.30
  49.9 14.1 copy-start.13
  51.0 0.8 copy-start.15
  52.3 10.6 collective-permute-start.3
  58.1 9.0 collective-permute-start.5
  63.5 3.6 collective-permute-start.4
  71.1 1.0 copy-start.7
  79.6 135.9 %copy-start.38 = (f32[128]{0:T(128)}, f32[128]{0:T(128)S(1)}, u32[]{:S(2)}) copy-start(f32[128]{0:T(128)S(1)} %add.103) | copy-start | bytes 1540
  408.9 4.3 copy-start.18
  413.2 1.6 copy-start.39
  413.2 1.6 copy-start.34
  424.9 5.9 copy-start.31
  426.4 3.4 collective-permute-start.6
  427.6 5.7 collective-permute-start.7
  429.8 3.6 collective-permute-start.8
  435.5 2.4 copy-start.33
  437.9 3.4 copy-start.3
  437.9 3.5 copy-start.5
  437.9 3.5 copy-start.27
  437.9 3.5 copy-start.32
  437.9 3.5 copy-start.37
  441.4 2.9 copy-start.11
  441.4 2.9 copy-start.29
  444.3 1.3 copy-start.21
  445.7 1.0 copy-start.16
  461.1 5.4 copy-start.25
  466.5 2.5 copy-start.22
  471.3 0.7 copy-start.35
  471.4 801.7 %reduce-scatter.3.cloned.1.call-start = ((), (), s32[]{:S(2)}) async-start(), calls=%async_computation.4 | async-start | bytes 8454144 | tf_op jit(solution)/shard_map/reduce_scatter | solution.py:151
  476.6 1.0 copy-start.17
  476.6 1.2 copy-start.23
  476.6 1462.2 %reduce-scatter.5.cloned.1.call-start = ((), (), s32[]{:S(2)}) async-start(), calls=%async_computation.5 | async-start | bytes 8454144 | tf_op jit(solution)/shard_map/reduce_scatter | solution.py:148
  487.3 5.6 copy-start.12
  492.9 8.4 copy-start.9
  492.9 8.4 copy-start.19
  495.6 5.0 collective-permute-start.9
  499.6 10.1 collective-permute-start.11
  500.6 9.1 collective-permute-start.10
  502.3 8.4 copy-start.8
  502.3 8.4 copy-start.14
  510.1 1428.8 %copy-start.1 = (bf16[512,512]{1,0:T(8,128)(2,1)S(1)}, bf16[512,512]{1,0:T(8,128)(2,1)}, u32[]{:S(2)}) copy-start(bf16[512,512]{1,0:T(8,128)(2,1)} %param.14) | copy-start | bytes 1572868
Sparse Core Ops, SparseCore 0:
  9.7 201.0 all-gather.4
  212.5 196.3 all-gather.2
  471.5 157.1 all-reduce.5
  631.4 641.6 reduce-scatter.2
  1276.0 662.8 reduce-scatter.4
where the time goes:
time: 1980 us; the launch traced here: 1950 us
  waiting for transfers between devices  1770 us (89%)
  local copies, waits for them, and re-layouts  76.8 us (4%)
  matrix products  44.7 us (2%)
  other arithmetic  23.6 us (1%)
  starting transfers between devices  19.8 us (1%)
    reduce_scatter x1, waiting for transfers between devices, per_device(): lax.psum_scatter(inner(coarse, merged_cot), ('lat', 'lon'), scatter_dimen...  666 us
    reduce_scatter x1, waiting for transfers between devices, per_device(): lax.psum_scatter(inner(merged_norm, grad_pre), ('lat', 'lon'), scatter_di...  642 us
    all_gather x1, waiting for transfers between devices, per_device(): merge_full = lax.all_gather(w_merge, ('lat', 'lon'), axis=0, tiled=True)  193 us
    all_gather x1, waiting for transfers between devices, per_device(): split_full = lax.all_gather(w_split, ('lat', 'lon'), axis=0, tiled=True)  131 us
    unnamed x6, waiting for transfers between devices  118 us
  transfers between devices with their start and end apart: 17, of which 14 were waited for; matrix products, arithmetic and copies ran while one was open for 4% of the time, Pallas kernels for 0%

commit v1 on v0

v1 whole, which is shorter than its diff:
```python
import functools

import jax
import jax.numpy as jnp
from jax import lax
from jax.experimental import pallas as pl
from jax.experimental.pallas import tpu as pltpu
from jax.sharding import Mesh, PartitionSpec as P

HEADS = 8
WIN = 8
SHIFT = 4
EPS_NORM = 1e-05
EPS_UNIT = 1e-06

D = 512
ROWS, COLS = 8, 64
WINS = COLS // WIN + 1
CELLS = 24
OWN = 16
PATCHES = 4 * CELLS
TOKENS = WINS * PATCHES
ALL_CELLS = WINS * CELLS
OWN_CELLS = WINS * OWN
LANES = 128
VMEM_BYTES = 48 * 1024 * 1024

AXES = ("xl", "xh", "z", "y", "c")
CHIP_AXES = ("xl", "xh", "z", "y")
LON = ("xh", "z", "y", "c")

F32 = jnp.float32
BF16 = jnp.bfloat16


def device_index(x, y, z, c):
    return ((((x % 2) * 2 + x // 2) * 4 + z) * 4 + y) * 2 + c


def move(value, x=0, y=0, z=0, c=0):
    pairs = []
    for px in range(4):
        for pz in range(4):
            for py in range(4):
                for pc in range(2):
                    target = ((px + x) % 4, (py + y) % 4, (pz + z) % 4, (pc + c) % 2)
                    pairs.append((device_index(px, py, pz, pc), device_index(*target)))
    return lax.ppermute(value, AXES, pairs)


def slide(value, lat, lon):
    pairs = []
    for row in range(2):
        for col in range(64):
            pairs.append((row * 64 + col, (row + lat) % 2 * 64 + (col + lon) % 64))
    return lax.ppermute(value, AXES, pairs)


def half_of(value, which):
    width = value.shape[-1] // 2
    return lax.dynamic_slice_in_dim(value, which * width, width, value.ndim - 1)


def join_cores(mine, other, core, axis):
    return jnp.where(
        core == 0,
        jnp.concatenate([mine, other], axis=axis),
        jnp.concatenate([other, mine], axis=axis),
    )


def gather(block, axes, count):
    copies = jnp.broadcast_to(block[None], (count,) + block.shape)
    return lax.all_to_all(copies, axes, 0, 0, tiled=True)


def scatter(blocks, axes):
    return jnp.sum(lax.all_to_all(blocks, axes, 0, 0, tiled=True).astype(F32), axis=0)


def own_rows(block, core):
    rows = block.shape[0] // 2
    mine = lax.dynamic_slice_in_dim(block, core * rows, rows, 0)
    other = move(lax.dynamic_slice_in_dim(block, (1 - core) * rows, rows, 0), c=1)
    return join_cores(mine, other, core, 1)


def inner(left, right):
    return lax.dot_general(left, right, (((0,), (0,)), ((), ())), preferred_element_type=F32)


def rims(field, lat):
    width = field.shape[-1]
    near = lax.dynamic_slice_in_dim(field, (1 - lat) * SHIFT, SHIFT, 0)
    out = [slide(near, 1, 0)]
    for step in (1, -1):
        cut = slice(COLS - SHIFT, COLS) if step == 1 else slice(0, SHIFT)
        out.append(slide(field[:, cut].reshape(-1, width), 0, step))
        out.append(slide(near[:, cut].reshape(-1, width), 1, step))
    return out


def dot(left, right):
    return jnp.dot(left, right, preferred_element_type=F32)


def dot_t(left, right):
    return lax.dot_general(left, right, (((1,), (1,)), ((), ())), preferred_element_type=F32)


def lay_out(wide, own, across, west, west_far, east, east_far, groups, skipped=0):
    sides = [
        (0, west[...].astype(F32), west_far[...].astype(F32)),
        (SHIFT + COLS, east[...].astype(F32), east_far[...].astype(F32)),
    ]
    for group in range(groups):
        lanes = slice(group * LANES, (group + 1) * LANES)
        rim_lanes = slice(skipped + group * LANES, skipped + (group + 1) * LANES)
        for row in range(ROWS + SHIFT):
            centre = own[row, :, lanes] if row < ROWS else across[row - ROWS, :, rim_lanes]
            wide[group, row, SHIFT : SHIFT + COLS, :] = centre.astype(F32)
            for start, close, far in sides:
                part, at = (close, row) if row < ROWS else (far, row - ROWS)
                wide[group, row, start : start + SHIFT, :] = part[SHIFT * at : SHIFT * (at + 1), rim_lanes]


def chunks(row_pairs):
    for win in range(WINS):
        for pair in range(row_pairs):
            for parity in range(4):
                row = 2 * pair + parity // 2
                yield win, pair, parity, row, pl.ds(WIN * win + parity % 2, 4, stride=2)


def give_back(out, wide):
    for group in range(4):
        lanes = slice(group * LANES, (group + 1) * LANES)
        for row in range(ROWS):
            out[row, :, lanes] = wide[group, row, SHIFT : SHIFT + COLS, :].astype(BF16)


def own_mask(per_window, shape):
    index = lax.broadcasted_iota(jnp.int32, shape, 0)
    win = index // per_window
    cell = (index % per_window) % (CELLS if per_window % CELLS == 0 else OWN)
    west = (win == 0) & (cell % 4 < 2)
    east = (win == WINS - 1) & (cell % 4 >= 2)
    return ((cell < OWN) & ~west & ~east).astype(F32)


def head_sums(values):
    row = lax.broadcasted_iota(jnp.int32, (D, D), 0) // 64
    col = lax.broadcasted_iota(jnp.int32, (D, D), 1) // 64
    same = (row == col).astype(BF16)
    high = values.astype(BF16)
    low = (values - high.astype(F32)).astype(BF16)
    return dot(high, same) + dot(low, same)


def normalize(values):
    centre = values - jnp.mean(values, axis=-1, keepdims=True)
    scale = lax.rsqrt(jnp.mean(centre * centre, axis=-1, keepdims=True) + EPS_NORM)
    return centre * scale, scale


def normalize_back(grad, normed, scale):
    mean = jnp.mean(grad, axis=-1, keepdims=True)
    slope = jnp.mean(grad * normed, axis=-1, keepdims=True)
    return scale * (grad - mean - normed * slope)


def lane_halves():
    lane = lax.broadcasted_iota(jnp.int32, (1, LANES), 1)
    return [(lane < 64).astype(BF16), (lane >= 64).astype(BF16)]


def fine_forward_kernel(
    spot, logit, own, across, west, west_far, east, east_far, table, w_qkv, w_out,
    skip, merged_norm, merged_spread, normed, spread, units, unit_scale, weights, attended,
    wide, embedded,
):
    lay_out(wide, own, across, west, west_far, east, east_far, 5)
    for win, pair, parity, row, cols in chunks(6):
        at = win * PATCHES + parity * CELLS + pair * 4
        for group in range(5):
            embedded[at : at + 4, group * LANES : (group + 1) * LANES] = wide[group, row, cols, :]

    @pl.loop(0, WINS)
    def _(win):
        rows = pl.ds(pl.multiple_of(win * PATCHES, 32), PATCHES)
        kind = embedded[rows, D : D + 1]
        first, second, third = table[0:1, :], table[1:2, :], table[2:3, :]
        added = jnp.where(kind == 0.0, first, jnp.where(kind == 1.0, second, third))
        values = embedded[rows, :D] + added
        embedded[rows, :D] = values
        unit, scale = normalize(values)
        normed[rows, :] = unit.astype(BF16)
        spread[rows, :] = scale

    block = TOKENS // 3
    for part in range(3):
        columns = slice(part * D, (part + 1) * D)
        for start in range(0, TOKENS, block):
            rows = slice(start, start + block)
            values = dot(normed[rows, :], w_qkv[:, columns])
            if part < 2:
                scale = lax.rsqrt(head_sums(values * values) + EPS_UNIT)
                unit_scale[rows, columns] = scale
                values = values * scale
            units[rows, columns] = values.astype(BF16)

    halves = lane_halves()
    outer = []
    for axis in range(2):
        index = lax.broadcasted_iota(jnp.int32, (PATCHES, PATCHES), axis)
        outer.append(((index % CELLS) // 8 == spot[0]).astype(jnp.int32))
    same = outer[0] == outer[1]

    @pl.loop(0, WINS)
    def _(win):
        rows = pl.ds(pl.multiple_of(win * PATCHES, 32), PATCHES)
        for duo in range(4):
            lanes = slice(duo * LANES, (duo + 1) * LANES)
            queries = units[rows, lanes]
            keys = units[rows, D + duo * LANES : D + (duo + 1) * LANES]
            values = units[rows, 2 * D + duo * LANES : 2 * D + (duo + 1) * LANES]
            total = jnp.zeros((PATCHES, LANES), F32)
            for side in range(2):
                head = 2 * duo + side
                scores = dot_t(queries, keys * halves[side]) * logit[head]
                exponent = jnp.where(same, jnp.exp(scores), 0.0)
                share = exponent * (1.0 / jnp.sum(exponent, axis=-1, keepdims=True))
                share = share.astype(BF16)
                weights[win * HEADS + head] = share
                total = total + dot(share, values * halves[side])
            attended[rows, lanes] = total.astype(BF16)

    for start in range(0, TOKENS, block):
        rows = slice(start, start + block)
        projected = dot(attended[rows, :], w_out[...]).astype(BF16).astype(F32)
        embedded[rows, :D] = (embedded[rows, :D] + projected).astype(BF16).astype(F32)
    for win in range(WINS):
        for parity in range(4):
            at = win * PATCHES + parity * CELLS
            skip[win * CELLS : (win + 1) * CELLS, parity * D : (parity + 1) * D] = embedded[
                at : at + CELLS, :D
            ]
    unit, scale = normalize(skip[...])
    merged_norm[...] = unit.astype(BF16)
    merged_spread[...] = scale


def cotangent_kernel(own, across, west, west_far, east, east_far, merged, rounded, wide):
    lay_out(wide, own, across, west, west_far, east, east_far, 4, D + LANES)
    for win, pair, parity, row, cols in chunks(6):
        at = win * CELLS + pair * 4
        for group in range(4):
            lane = parity * D + group * LANES
            merged[at : at + 4, lane : lane + LANES] = wide[group, row, cols, :]
    rounded[...] = merged[...].astype(BF16)


def coarse_kernel(
    norm, norm_other, cot, cot_other, parts, coarse, grad_pre, split, blocks, merge, sem
):
    copy = pltpu.make_async_copy(parts, merge, sem)
    copy.start()
    copy.wait()
    w_merge = merge[:, :32, :].reshape(2048, 512)
    for j in range(2):
        pair = merge[:, 32 + 16 * j : 48 + 16 * j, :].astype(F32)
        for k in range(2):
            quarter = pair[:, 8 * k : 8 * k + 8, :].reshape(512, 512)
            column = (2 * j + k) * 512
            split[:, column : column + 512] = quarter.astype(BF16)
    slope = 0.7978845608028654
    cubic = 0.044715
    keep = own_mask(CELLS, (ALL_CELLS, 1))
    own_grads, own_cots = [], []
    for i, (unit, cotangent) in enumerate(((norm, cot), (norm_other, cot_other))):
        value = dot(unit[...], w_merge)
        square = value * value
        bend = jnp.tanh(slope * (value + cubic * (square * value)))
        half_bend = 0.5 * (1.0 + bend)
        coarse[i] = (value * half_bend).astype(BF16)
        rise = half_bend + 0.5 * value * (1.0 - bend * bend) * slope * (1.0 + 3.0 * cubic * square)
        grad = dot_t(cotangent[...], split[...]) * rise
        grad_pre[i] = grad.astype(BF16)
        own_grads.append((grad * keep).astype(BF16))
        own_cots.append((coarse[i].astype(F32) * keep).astype(BF16))
    for x in range(4):
        chips = slice(x * 16, (x + 1) * 16)
        lanes = slice(x * 512, (x + 1) * 512)
        block = inner(norm[:, lanes], own_grads[0]) + inner(norm_other[:, lanes], own_grads[1])
        blocks[chips, :32, :] = block.astype(BF16).reshape(16, 32, 512)
    for j in range(2):
        quarters = []
        for k in range(2):
            lanes = slice((2 * j + k) * 512, (2 * j + k + 1) * 512)
            block = inner(own_cots[0], cot[:, lanes]) + inner(own_cots[1], cot_other[:, lanes])
            quarters.append(block.reshape(64, 8, 512))
        pair = jnp.concatenate(quarters, axis=1).astype(BF16)
        blocks[:, 32 + 16 * j : 48 + 16 * j, :] = pair


def partial_kernel(
    parts, coarse, grad_pre, split, grad_mine, grad_other, out_mine, out_other, merge, sem
):
    copy = pltpu.make_async_copy(parts.at[:, :32], merge, sem)
    copy.start()
    for i, out in enumerate((out_mine, out_other)):
        out[...] = dot(coarse[i], split[...]).astype(out.dtype)
    copy.wait()
    w_merge = merge[...].reshape(2048, 512)
    for i, out in enumerate((grad_mine, grad_other)):
        out[...] = dot_t(grad_pre[i], w_merge).astype(out.dtype)


def decode_kernel(skip, out_mine, received, decoded, sum_m, wide):
    sum_m[...] = skip[...] + out_mine[...] + received[...].astype(F32)
    for win, pair, parity, row, cols in chunks(4):
        at = win * CELLS + pair * 4
        for group in range(4):
            lane = parity * D + group * LANES
            wide[group, row, cols, :] = sum_m[at : at + 4, lane : lane + LANES]
    give_back(decoded, wide)


def fine_backward_kernel(
    spot, logit, grad_mine, received, cot, merged_norm, merged_spread,
    units, unit_scale, weights, normed, attended, w_out,
    grad_skip, grad_packed, grads_mine, grads_other,
    grad_tokens, grad_att, grad_units,
):
    grad = (grad_mine[...] + received[...].astype(F32)).astype(BF16).astype(F32)
    grad_skip[...] = cot[...] + normalize_back(grad, merged_norm[...].astype(F32), merged_spread[...])
    for win in range(WINS):
        for parity in range(4):
            at = win * PATCHES + parity * CELLS
            grad_tokens[at : at + CELLS, :] = grad_skip[
                win * CELLS : (win + 1) * CELLS, parity * D : (parity + 1) * D
            ]
    block = TOKENS // 3
    for start in range(0, TOKENS, block):
        rows = slice(start, start + block)
        grad_att[rows, :] = dot_t(grad_tokens[rows, :].astype(BF16), w_out[...]).astype(BF16)
    halves = lane_halves()

    @pl.loop(0, WINS)
    def _(win):
        rows = pl.ds(pl.multiple_of(win * PATCHES, 32), PATCHES)
        for duo in range(4):
            lanes = slice(duo * LANES, (duo + 1) * LANES)
            key_lanes = slice(D + duo * LANES, D + (duo + 1) * LANES)
            value_lanes = slice(2 * D + duo * LANES, 2 * D + (duo + 1) * LANES)
            queries, keys, values = units[rows, lanes], units[rows, key_lanes], units[rows, value_lanes]
            grad_out = grad_att[rows, lanes]
            grad_q = jnp.zeros((PATCHES, LANES), F32)
            grad_k = jnp.zeros((PATCHES, LANES), F32)
            grad_v = jnp.zeros((PATCHES, LANES), F32)
            for side in range(2):
                head = 2 * duo + side
                half = halves[side]
                share = weights[win * HEADS + head]
                wide_share = share.astype(F32)
                flow = dot_t(grad_out, values * half) * wide_share
                flow = flow - wide_share * jnp.sum(flow, axis=-1, keepdims=True)
                flow = (flow * logit[head]).astype(BF16)
                grad_q = grad_q + dot(flow, keys * half)
                grad_k = grad_k + inner(flow, queries * half)
                grad_v = grad_v + inner(share, grad_out * half)
            grad_units[rows, lanes] = grad_q
            grad_units[rows, key_lanes] = grad_k
            grad_packed[rows, value_lanes] = grad_v.astype(BF16)

    for part in range(2):
        columns = slice(part * D, (part + 1) * D)
        for start in range(0, TOKENS, block):
            rows = slice(start, start + block)
            unit = units[rows, columns].astype(F32)
            grad = grad_units[rows, columns]
            along = head_sums(unit * grad)
            grad_packed[rows, columns] = (
                unit_scale[rows, columns] * (grad - unit * along)
            ).astype(BF16)
    keep = own_mask(PATCHES, (TOKENS, 1))
    own_grad = (grad_tokens[...] * keep).astype(BF16)
    own_normed = (normed[...].astype(F32) * keep).astype(BF16)
    for part in range(4):
        if part < 3:
            result = inner(own_normed, grad_packed[:, part * D : (part + 1) * D]).astype(BF16)
        else:
            result = inner(attended[...], own_grad).astype(BF16)
        lanes = slice(part % 2 * D, (part % 2 + 1) * D)

        @pl.when(spot[1] == part // 2)
        def _():
            grads_mine[:, lanes] = result

        @pl.when(spot[1] != part // 2)
        def _():
            grads_other[:, lanes] = result


def field_grad_kernel(grad_skip, grad_packed, normed, spread, w_qkv, grad_fields, total, wide):
    block = TOKENS // 3
    for start in range(0, TOKENS, block):
        rows = slice(start, start + block)
        grad = dot_t(grad_packed[rows, :], w_qkv[...]).astype(BF16).astype(F32)
        total[rows, :] = normalize_back(grad, normed[rows, :].astype(F32), spread[rows, :])
    for win, pair, parity, row, cols in chunks(4):
        at = win * PATCHES + parity * CELLS + pair * 4
        cell = win * CELLS + pair * 4
        for group in range(4):
            lanes = slice(group * LANES, (group + 1) * LANES)
            lane = parity * D + group * LANES
            wide[group, row, cols, :] = (
                total[at : at + 4, lanes] + grad_skip[cell : cell + 4, lane : lane + LANES]
            )
    give_back(grad_fields, wide)


def kernel_call(
    kernel, name, outs, scratch, args, scalars=0, ahead=0, in_place=0, flops=0, moved=0, curves=0
):
    count = len(args)
    specs = []
    for index in range(count):
        if index < scalars:
            specs.append(pl.BlockSpec(memory_space=pltpu.SMEM))
        elif index < ahead or index >= count - in_place:
            specs.append(pl.BlockSpec(memory_space=pl.ANY))
        else:
            specs.append(pl.BlockSpec(memory_space=pltpu.VMEM))
    shapes = [jax.ShapeDtypeStruct(shape, dtype) for shape, dtype in outs]
    return pl.pallas_call(
        kernel,
        out_shape=shapes,
        in_specs=specs,
        out_specs=[pl.BlockSpec(memory_space=pltpu.VMEM)] * len(outs),
        scratch_shapes=scratch,
        compiler_params=pltpu.CompilerParams(vmem_limit_bytes=VMEM_BYTES),
        cost_estimate=pl.CostEstimate(flops=flops, bytes_accessed=moved, transcendentals=curves),
        name=name,
    )(*args)


def per_device(
    fields, surface, surface_table, logit_scale, w_qkv, w_out, w_merge, w_split, cotangent
):
    core = lax.axis_index("c")
    lat = lax.axis_index("xl")
    spot = jnp.stack([lat, core]).astype(jnp.int32)
    kinds = jnp.broadcast_to(surface.astype(BF16)[:, :, None], (ROWS, COLS, LANES))
    own_fields = jnp.concatenate([fields, kinds], axis=-1)
    rim = rims(jnp.concatenate([own_fields, cotangent], axis=-1), lat)

    index = jnp.arange(1024, dtype=jnp.int32)
    source = index % 512 // 8 * 16 + index // 512 * 8 + index % 8
    runs = (index[:, None] == source[None, :]).astype(BF16)
    sorted_merge = jnp.dot(w_merge, runs, preferred_element_type=F32).astype(BF16)
    far = move(half_of(sorted_merge, 1 - core), c=1)
    merge_block = join_cores(half_of(sorted_merge, core), far, core, 0)
    split_block = w_split.reshape(8, 4, 512).transpose(1, 0, 2).reshape(32, 512)
    block = jnp.concatenate([merge_block, split_block], axis=0)
    *rim, block = lax.optimization_barrier((*rim, block))
    mine = gather(block, CHIP_AXES, 64)

    cells = (ALL_CELLS, 4 * D)
    skip, merged_norm, merged_spread, normed, spread, units, unit_scale, weights, attended = kernel_call(
        fine_forward_kernel,
        "fine_forward",
        [
            (cells, F32),
            (cells, BF16),
            ((ALL_CELLS, 1), F32),
            ((TOKENS, D), BF16),
            ((TOKENS, 1), F32),
            ((TOKENS, 3 * D), BF16),
            ((TOKENS, 2 * D), F32),
            ((WINS * HEADS, PATCHES, PATCHES), BF16),
            ((TOKENS, D), BF16),
        ],
        [pltpu.VMEM((5, 12, 72, LANES), F32), pltpu.VMEM((TOKENS, D + LANES), F32)],
        (spot, logit_scale, own_fields, *rim, surface_table, w_qkv, w_out),
        scalars=2,
        flops=15_000_000_000,
        moved=12_000_000,
    )
    cot, cot_rounded = kernel_call(
        cotangent_kernel,
        "cotangent_cells",
        [(cells, F32), (cells, BF16)],
        [pltpu.VMEM((4, 12, 72, LANES), F32)],
        (cotangent, *rim),
        moved=8_000_000,
    )
    norm_other, cot_other = move(merged_norm, c=1), move(cot_rounded, c=1)
    norm_other, cot_other, mine = lax.optimization_barrier((norm_other, cot_other, mine))
    coarse, grad_pre, split, blocks = kernel_call(
        coarse_kernel,
        "coarse",
        [
            ((2, ALL_CELLS, 512), BF16),
            ((2, ALL_CELLS, 512), BF16),
            ((512, 2048), BF16),
            ((64, 64, 512), BF16),
        ],
        [pltpu.VMEM((64, 64, 512), BF16), pltpu.SemaphoreType.DMA],
        (merged_norm, norm_other, cot_rounded, cot_other, mine),
        in_place=1,
        flops=8_000_000_000,
        moved=15_000_000,
    )
    split, blocks = lax.optimization_barrier((split, blocks))
    blocks = scatter(blocks, CHIP_AXES)
    grad_mine, grad_other, out_mine, out_other = kernel_call(
        partial_kernel,
        "partial_products",
        [(cells, F32), (cells, BF16), (cells, F32), (cells, BF16)],
        [pltpu.VMEM((64, 32, 512), BF16), pltpu.SemaphoreType.DMA],
        (mine, coarse, grad_pre, split),
        ahead=1,
        flops=3_000_000_000,
        moved=10_000_000,
    )
    grad_skip, grad_packed, fine_mine, fine_other = kernel_call(
        fine_backward_kernel,
        "fine_backward",
        [(cells, F32), ((TOKENS, 3 * D), BF16), ((D, 1024), BF16), ((D, 1024), BF16)],
        [
            pltpu.VMEM((TOKENS, D), F32),
            pltpu.VMEM((TOKENS, D), BF16),
            pltpu.VMEM((TOKENS, 2 * D), F32),
        ],
        (
            spot,
            logit_scale,
            grad_mine,
            move(grad_other, c=1),
            cot,
            merged_norm,
            merged_spread,
            units,
            unit_scale,
            weights,
            normed,
            attended,
            w_out,
        ),
        scalars=2,
        flops=15_000_000_000,
        moved=15_000_000,
    )
    (decoded,) = kernel_call(
        decode_kernel,
        "decode",
        [((ROWS, COLS, D), BF16)],
        [pltpu.VMEM(cells, F32), pltpu.VMEM((4, 8, 72, LANES), F32)],
        (skip, out_mine, move(out_other, c=1)),
        moved=8_000_000,
    )
    (grad_fields,) = kernel_call(
        field_grad_kernel,
        "field_grad",
        [((ROWS, COLS, D), BF16)],
        [pltpu.VMEM((TOKENS, D), F32), pltpu.VMEM((4, 8, 72, LANES), F32)],
        (grad_skip, grad_packed, normed, spread, w_qkv),
        flops=4_000_000_000,
        moved=8_000_000,
    )
    fine_half = (fine_mine.astype(F32) + move(fine_other, c=1).astype(F32)).astype(BF16)
    fine_half, blocks = lax.optimization_barrier((fine_half, blocks))
    fine_grads = own_rows(scatter(fine_half.reshape(64, D // 64, 1024), CHIP_AXES), core)
    grad_split = blocks[32:].reshape(4, 8, 512).transpose(1, 0, 2).reshape(8, 2048)
    grad_merge = own_rows(blocks[:32], core).reshape(16, 2, 64, 8).transpose(0, 2, 1, 3)
    return (
        decoded,
        grad_fields,
        fine_grads[:, : 3 * D],
        fine_grads[:, 3 * D :],
        grad_merge.reshape(16, 1024),
        grad_split,
    )


def solution(mesh):
    fine_mesh = Mesh(mesh.devices.reshape(2, 2, 4, 4, 2), AXES)
    grid, rows = P("xl", LON, None), P(AXES, None)
    in_specs = (grid, P("xl", LON), P(), P(), P(), P(), rows, rows, grid)
    out_specs = (grid, grid, rows, rows, rows, rows)
    return jax.shard_map(
        per_device, mesh=fine_mesh, in_specs=in_specs, out_specs=out_specs, check_vma=False
    )
```

time: 1980 us -> 205 us (0.10); the launches traced: 1950 us -> 204 us
  waiting for transfers between devices: 1770 us -> 37.9 us
  Pallas kernels: 0 us -> 68.7 us
  local copies, waits for them, and re-layouts: 76.8 us -> 23.9 us
  matrix products: 44.7 us -> 0.74 us
  starting transfers between devices: 19.8 us -> 63.6 us
    reduce_scatter x2 -> x0, waiting for transfers between devices: 1310 us -> none  [the longest x1 666 us: per_device(): lax.psum_scatter(inner(coarse, merged_cot), ('lat', 'lon'), scatter_dimen...]
    all_gather x2 -> x0, waiting for transfers between devices: 324 us -> none  [the longest x1 193 us: per_device(): merge_full = lax.all_gather(w_merge, ('lat', 'lon'), axis=0, tiled=True)]
    unnamed x6 -> x0, waiting for transfers between devices: 118 us -> none
    pallas_call x0 -> x7, Pallas kernels: none -> 68.7 us  [kernel_call(): pl.pallas_call(kernel, out_shape=shapes, in_specs=specs, out_specs=[pl.Bl...]
    dot_general x19 -> x1, matrix products: 44.7 us -> 0.74 us  [per_device(): jnp.dot(w_merge, runs, preferred_element_type=F32).astype(BF16)]
    all_to_all x0 -> x3, starting transfers between devices: none -> 42.4 us  [the longest x2 23.8 us: scatter(): lax.all_to_all(blocks, axes, 0, 0, tiled=True).astype(F32)]
    all_to_all x0 -> x3, waiting for transfers between devices: none -> 29.7 us  [the longest x1 15.7 us: gather(): return lax.all_to_all(copies, axes, 0, 0, tiled=True)]
    convert_element_type x7 -> x0, local copies, waits for them, and re-layouts: 21.6 us -> none  [the longest x3 14.5 us: per_device(): grad_packed.reshape(token_count, 3 * model_width).astype(jnp.bfloat16)]
  transfers between devices with their start and end apart: 17 -> 16, of which waited for: 14 -> 9; matrix products, arithmetic and copies ran while one was open for 4% -> 3% of each run, Pallas kernels for 0% -> 29%
where the time goes in v1:
time: 205 us; the launch traced here: 204 us
  Pallas kernels  68.7 us (34%)
  starting transfers between devices  63.6 us (31%)
  waiting for transfers between devices  37.9 us (18%)
  local copies, waits for them, and re-layouts  23.9 us (12%)
  other arithmetic  7.83 us (4%)
    pallas_call x7, Pallas kernels, kernel_call(): pl.pallas_call(kernel, out_shape=shapes, in_specs=specs, out_specs=[pl.Bl...  68.7 us
    all_to_all x2, starting transfers between devices, scatter(): lax.all_to_all(blocks, axes, 0, 0, tiled=True).astype(F32)  23.8 us
    all_to_all x1, starting transfers between devices, gather(): return lax.all_to_all(copies, axes, 0, 0, tiled=True)  18.6 us
    unnamed x57, local copies, waits for them, and re-layouts  18.4 us
    all_to_all x1, waiting for transfers between devices, gather(): return lax.all_to_all(copies, axes, 0, 0, tiled=True)  15.7 us
    all_to_all x2, waiting for transfers between devices, scatter(): lax.all_to_all(blocks, axes, 0, 0, tiled=True).astype(F32)  14 us
    ppermute x8, starting transfers between devices, move(): return lax.ppermute(value, AXES, pairs)  11.8 us
    ppermute x5, starting transfers between devices, slide(): return lax.ppermute(value, AXES, pairs)  9.48 us
  transfers between devices with their start and end apart: 16, of which 9 were waited for; matrix products, arithmetic and copies ran while one was open for 3% of the time, Pallas kernels for 29%

profile of v1, /device:TPU:1, one launch (start us, length us, event | category | flops | bytes accessed | tf_op | source)
XLA Modules:
  0.0 203.7 jit_solution(10898426362550456975)
XLA Ops:
  0.7 0.7 copy-done
  1.4 0.7 fusion.2
  2.1 1.5 collective-permute-start.5
  3.6 0.7 convert_element_type.23
  4.3 0.1 broadcast_in_dim.4
  4.5 1.4 pad_maximum_fusion
  5.9 2.3 %collective-permute-start.2 = (bf16[16,1152]{1,0:T(8,128)(2,1)S(1)}, bf16[16,1152]{1,0:T(8,128)(2,1)S(1)}, u32[]{:S(2)}, u32[]{:S(2)}) collective-permute-start(bf16[16,1152]{1,0:T(8,128)(2,1)S(1)} %reshape.96), channel_id=1, source_target_pairs={{0,65},{1,66},{2,67},{3,68},{4,69},{5,70},{6,71},{7,72},{8,73},{9,... | collective-permute-start | bytes 110600 | tf_op jit(solution)/shard_map/ppermute | solution.py:56
  8.4 0.9 collective-permute-start
  9.3 2.5 %collective-permute-start.1 = (bf16[32,1152]{1,0:T(8,128)(2,1)S(1)}, bf16[32,1152]{1,0:T(8,128)(2,1)S(1)}, u32[]{:S(2)}, u32[]{:S(2)}) collective-permute-start(bf16[32,1152]{1,0:T(8,128)(2,1)S(1)} %reshape.95), channel_id=1, source_target_pairs={{0,1},{1,2},{2,3},{3,4},{4,5},{5,6},{6,7},{7,8},{8,9},{9,10},{10,1... | collective-permute-start | bytes 221192 | tf_op jit(solution)/shard_map/ppermute | solution.py:56
  11.8 3.8 %collective-permute-start.3 = (bf16[32,1152]{1,0:T(8,128)(2,1)S(1)}, bf16[32,1152]{1,0:T(8,128)(2,1)S(1)}, u32[]{:S(2)}, u32[]{:S(2)}) collective-permute-start(bf16[32,1152]{1,0:T(8,128)(2,1)S(1)} %reshape.97), channel_id=1, source_target_pairs={{0,63},{1,0},{2,1},{3,2},{4,3},{5,4},{6,5},{7,6},{8,7},{9,8},{10,9... | collective-permute-start | bytes 221192 | tf_op jit(solution)/shard_map/ppermute | solution.py:56
  15.7 0.6 collective-permute-done.1.west
  16.3 0.3 collective-permute-done.3.east
  16.5 0.7 collective-permute-done.across
  17.2 2.5 %broadcast_in_dim.5 = bf16[64,64,512]{2,1,0:T(8,128)(2,1)} broadcast(bf16[64,512]{1,0:T(8,128)(2,1)S(1)} %pad_maximum_fusion.2), dimensions={1,2} | broadcast | bytes 4259840 | tf_op jit(solution)/shard_map/broadcast_in_dim | solution.py:73
  19.7 18.6 %all-to-all-start = ((bf16[64,64,512]{2,1,0:T(8,128)(2,1)}), bf16[64,64,512]{2,1,0:T(8,128)(2,1)}, u32[]{:S(2)}, u32[]{:S(2)}) async-start(bf16[64,64,512]{2,1,0:T(8,128)(2,1)} %broadcast_in_dim.5), calls=%async_computation | async-start | bytes 8388608 | tf_op jit(solution)/shard_map/all_to_all | solution.py:74
  38.5 0.6 cotangent_cells.1
  39.2 1.2 copy-done.3
  40.4 2.8 %collective-permute-start.7 = (bf16[216,2048]{1,0:T(8,128)(2,1)S(1)}, bf16[216,2048]{1,0:T(8,128)(2,1)S(1)}, u32[]{:S(2)}, u32[]{:S(2)}) collective-permute-start(bf16[216,2048]{1,0:T(8,128)(2,1)S(1)} %get-tuple-element.49.cot), channel_id=1, source_target_pairs={{0,1},{1,0},{2,3},{3,2},{4,5},{5,4},{6,7},{7,6},{8,9},{9,8},{10,11... | collective-permute-start | bytes 2654216 | tf_op jit(solution)/shard_map/ppermute | solution.py:48
  43.2 22.4 %fine_forward.1 = (f32[216,2048]{1,0:T(8,128)}, bf16[216,2048]{1,0:T(8,128)(2,1)S(1)}, f32[216,1]{1,0:T(8,128)S(1)}, bf16[864,512]{1,0:T(8,128)(2,1)S(1)}, f32[8...) custom-call(s32[2]{0:T(128)S(1)} %pad_add_fusion.spot, ...), custom_call_target="tpu_custom_call" | custom-call | flops 15000000512 | bytes 12000000 | tf_op jit(solution)/shard_map/fine_forward/pallas_call | solution.py:436
  65.6 0.9 copy-done.19
  66.6 0.8 copy-done.22
  67.3 0.9 copy-done.24
  68.2 0.3 collective-permute-start.6
  68.5 2.1 %collective-permute-done.6.norm_other = bf16[216,2048]{1,0:T(8,128)(2,1)S(1)} collective-permute-done((bf16[216,2048]{1,0:T(8,128)(2,1)S(1)}, bf16[216,2048]{1,0:T(8,128)(2,1)S(1)}, u32[]{:S(2)}, u32[]{:S(2)}) %collective-permute-start.6) | collective-permute-done | bytes 884768 | tf_op jit(solution)/shard_map/ppermute | solution.py:48
  70.7 0.9 copy-done.8
  71.6 15.7 %all-to-all-done.parts = bf16[64,64,512]{2,1,0:T(8,128)(2,1)} async-done(((bf16[64,64,512]{2,1,0:T(8,128)(2,1)}), bf16[64,64,512]{2,1,0:T(8,128)(2,1)}, u32[]{:S(2)}, u32[]{:S(2)}) %all-to-all-start) | async-done | bytes 4194336 | tf_op jit(solution)/shard_map/all_to_all | solution.py:74
  87.3 1.2 copy-done.7
  88.5 1.2 copy-done.9
  89.6 9.4 %coarse.1 = (bf16[2,216,512]{2,1,0:T(8,128)(2,1)S(1)}, bf16[2,216,512]{2,1,0:T(8,128)(2,1)S(1)}, bf16[512,2048]{1,0:T(8,128)(2,1)}, bf16[64,64,512]{2,1,0:T(8,128)(2,1)}) custom-call(bf16[216,2048]{1,0:T(8,128)(2,1)S(1)} %get-tuple-element.48.norm.merged_norm, bf16[216,2048]{1,0:T(8,128)(2,1)S(1)} %copy-done.9, bf16[216,2048]{1,0:T(8,128)(2,1)S(1)} %copy-done.7, ...), custom_call_target="tpu_custom_call" | custom-call | flops 8000000000 | bytes 15000000 | tf_op jit(solution)/shard_map/coarse/pallas_call | solution.py:436
  99.1 0.8 copy-done.15
  99.8 0.8 copy-done.17
  100.6 14.7 %all-to-all-start.1 = ((bf16[64,64,512]{2,1,0:T(8,128)(2,1)}), bf16[64,64,512]{2,1,0:T(8,128)(2,1)}, u32[]{:S(2)}, u32[]{:S(2)}) async-start(bf16[64,64,512]{2,1,0:T(8,128)(2,1)} %get-tuple-element.75), calls=%async_computation.1 | async-start | bytes 8388608 | tf_op jit(solution)/shard_map/all_to_all | solution.py:78
  115.3 1.0 copy-done.16
  116.3 1.0 copy-done.18
  117.3 4.7 %partial_products.1 = (f32[216,2048]{1,0:T(8,128)S(1)}, bf16[216,2048]{1,0:T(8,128)(2,1)S(1)}, f32[216,2048]{1,0:T(8,128)S(1)}, bf16[216,2048]{1,0:T(8,128)(2,1)S(1)}) custom-call(bf16[64,64,512]{2,1,0:T(8,128)(2,1)} %all-to-all-done.parts, bf16[2,216,512]{2,1,0:T(8,128)(2,1)S(1)} %copy-done.16, bf16[2,216,512]{2,1,0:T(8,128)(2,1)S(1)} %copy-done.18, ...), custom_call_target="tpu_custom_call" | custom-call | flops 3000000000 | bytes 10000000 | tf_op jit(solution)/shard_map/partial_products/pallas_call | solution.py:436
  122.1 0.9 copy-done.5
  123.0 1.2 copy-done.13
  124.2 1.0 collective-permute-start.9
  125.2 2.1 %collective-permute-done.9.received = bf16[216,2048]{1,0:T(8,128)(2,1)S(1)} collective-permute-done((bf16[216,2048]{1,0:T(8,128)(2,1)S(1)}, bf16[216,2048]{1,0:T(8,128)(2,1)S(1)}, u32[]{:S(2)}, u32[]{:S(2)}) %collective-permute-start.9) | collective-permute-done | bytes 884768 | tf_op jit(solution)/shard_map/ppermute | solution.py:48
  127.3 25.4 %fine_backward.1 = (f32[216,2048]{1,0:T(8,128)}, bf16[864,1536]{1,0:T(8,128)(2,1)}, bf16[512,1024]{1,0:T(8,128)(2,1)S(1)}, bf16[512,1024]{1,0:T(8,128)(2,1)}) custom-call(s32[2]{0:T(128)S(1)} %pad_add_fusion.spot, f32[8]{0:T(128)S(1)} %copy-done.12, f32[216,2048]{1,0:T(8,128)} %copy-done.13, bf16[216,2048]{1,0:T(8,128)(2,1)S(1)} %collective-permute-done.9.received, ...), custom_call_target="tpu_custom_call" | custom-call | flops 15000000512 | bytes 15000000 | tf_op jit(solution)/shard_map/fine_backward/pallas_call | solution.py:436
  152.7 0.4 collective-permute-start.10
  153.0 2.5 %collective-permute-done.10 = bf16[512,1024]{1,0:T(8,128)(2,1)S(1)} collective-permute-done((bf16[512,1024]{1,0:T(8,128)(2,1)}, bf16[512,1024]{1,0:T(8,128)(2,1)S(1)}, u32[]{:S(2)}, u32[]{:S(2)}) %collective-permute-start.10) | collective-permute-done | bytes 1048608 | tf_op jit(solution)/shard_map/ppermute | solution.py:48
  155.5 1.4 add_convert_fusion
  156.9 11.5 %all-to-all-done.1 = bf16[64,64,512]{2,1,0:T(8,128)(2,1)} async-done(((bf16[64,64,512]{2,1,0:T(8,128)(2,1)}), bf16[64,64,512]{2,1,0:T(8,128)(2,1)}, u32[]{:S(2)}, u32[]{:S(2)}) %all-to-all-start.1) | async-done | bytes 4194336 | tf_op jit(solution)/shard_map/all_to_all | solution.py:78
  168.4 2.8 %convert_reduce_fusion = f32[64,512]{1,0:T(8,128)S(1)} fusion(bf16[64,64,512]{2,1,0:T(8,128)(2,1)} %all-to-all-done.1), kind=kLoop, calls=%fused_computation | loop fusion | flops 4161536 | bytes 4325376 | tf_op jit(solution)/shard_map/reduce_sum | solution.py:78
  171.3 9.1 %all-to-all-start.2 = ((bf16[64,8,1024]{2,1,0:T(8,128)(2,1)}), bf16[64,8,1024]{2,1,0:T(8,128)(2,1)}, u32[]{:S(2)}, u32[]{:S(2)}) async-start(bf16[64,8,1024]{2,1,0:T(8,128)(2,1)} %bitcast.7), calls=%async_computation.2 | async-start | bytes 2097152 | tf_op jit(solution)/shard_map/all_to_all | solution.py:78
  180.4 1.9 collective-permute-start.8
  182.3 0.6 fusion.26
  182.9 1.4 copy-done.4
  184.4 1.5 copy-done.14
  185.8 1.2 copy-done.21
  187.0 4.7 %field_grad.1 = bf16[8,64,512]{2,1,0:T(8,128)(2,1)} custom-call(f32[216,2048]{1,0:T(8,128)S(1)} %copy-done.14, bf16[864,1536]{1,0:T(8,128)(2,1)} %get-tuple-element.71.grad_packed, bf16[864,512]{1,0:T(8,128)(2,1)S(1)} %copy-done.21, f32[864,1]{1,0:T(8,128)S(1)} %copy-done.23, bf16[512,1536]{1,0:T(8,128)(2,1)S(1)} %copy-done.4), custom_call_target="tpu_custom_call" | custom-call | flops 4000000000 | bytes 8000000 | tf_op jit(solution)/shard_map/field_grad/pallas_call | solution.py:436
  191.7 1.4 decode.1
  193.1 0.1 copy.22
  193.3 0.1 copy.24
  193.4 0.1 copy.23
  193.5 0.1 copy.25
  193.7 2.4 %all-to-all-done.2 = bf16[64,8,1024]{2,1,0:T(8,128)(2,1)} async-done(((bf16[64,8,1024]{2,1,0:T(8,128)(2,1)}), bf16[64,8,1024]{2,1,0:T(8,128)(2,1)}, u32[]{:S(2)}, u32[]{:S(2)}) %all-to-all-start.2) | async-done | bytes 1048608 | tf_op jit(solution)/shard_map/all_to_all | solution.py:78
  196.1 1.4 convert_reduce_fusion.1
  197.5 3.9 %collective-permute-start.11 = (f32[4,1024]{1,0:T(4,128)S(1)}, f32[4,1024]{1,0:T(4,128)S(1)}, u32[]{:S(2)}, u32[]{:S(2)}) collective-permute-start(f32[4,1024]{1,0:T(4,128)S(1)} %get-tuple-element.105), channel_id=1, source_target_pairs={{0,1},{1,0},{2,3},{3,2},{4,5},{5,4},{6,7},{7,6},{8,9},{9,8},{10,11... | collective-permute-start | bytes 49160 | tf_op jit(solution)/shard_map/ppermute | solution.py:48
  201.4 0.3 copy.28
  201.7 0.8 copy.29
  202.5 0.6 slice.34
  203.1 0.6 slice.35
  (65 shorter events, 0.6 us)
Async XLA Ops:
  0.6 0.8 copy-start
  2.1 9.7 %collective-permute-start.5 = (bf16[16,512]{1,0:T(8,128)(2,1)S(1)}, bf16[16,512]{1,0:T(8,128)(2,1)S(1)}, u32[]{:S(2)}, u32[]{:S(2)}) collective-permute-start(bf16[16,512]{1,0:T(8,128)(2,1)S(1)} %get-tuple-element.107), channel_id=1, source_target_pairs={{0,1},{1,0},{2,3},{3,2},{4,5},{5,4},{6,7},{7,6},{8,9},{9,8},{10,11... | collective-permute-start | bytes 49160 | tf_op jit(solution)/shard_map/ppermute | solution.py:48
  4.5 11.2 %copy-start.27 = (bf16[8,2048]{1,0:T(8,128)(2,1)S(1)}, bf16[8,2048]{1,0:T(8,128)(2,1)}, u32[]{:S(2)}) copy-start(bf16[8,2048]{1,0:T(8,128)(2,1)} %param.16) | copy-start | bytes 98308
  5.9 9.7 %collective-permute-start.2 = (bf16[16,1152]{1,0:T(8,128)(2,1)S(1)}, bf16[16,1152]{1,0:T(8,128)(2,1)S(1)}, u32[]{:S(2)}, u32[]{:S(2)}) collective-permute-start(bf16[16,1152]{1,0:T(8,128)(2,1)S(1)} %reshape.96), channel_id=1, source_target_pairs={{0,65},{1,66},{2,67},{3,68},{4,69},{5,70},{6,71},{7,72},{8,73},{9,... | collective-permute-start | bytes 110600 | tf_op jit(solution)/shard_map/ppermute | solution.py:56
  8.2 7.4 %collective-permute-start.4 = (bf16[16,1152]{1,0:T(8,128)(2,1)S(1)}, bf16[16,1152]{1,0:T(8,128)(2,1)S(1)}, u32[]{:S(2)}, u32[]{:S(2)}) collective-permute-start(bf16[16,1152]{1,0:T(8,128)(2,1)S(1)} %reshape.98), channel_id=1, source_target_pairs={{0,127},{1,64},{2,65},{3,66},{4,67},{5,68},{6,69},{7,70},{8,71},{9... | collective-permute-start | bytes 110600 | tf_op jit(solution)/shard_map/ppermute | solution.py:56
  8.4 8.8 %collective-permute-start = (bf16[4,64,1152]{2,1,0:T(8,128)(2,1)S(1)}, bf16[4,64,1152]{2,1,0:T(8,128)(2,1)S(1)}, u32[]{:S(2)}, u32[]{:S(2)}) collective-permute-start(bf16[4,64,1152]{2,1,0:T(8,128)(2,1)S(1)} %constant_dynamic-slice_fusion.6), channel_id=1, source_target_pairs={{0,64},{1,65},{2,66},{3,67},{4,68},{5,69},{6,70},{7,71},{8,72},{9,... | collective-permute-start | bytes 1769480 | tf_op jit(solution)/shard_map/ppermute | solution.py:56
  9.3 6.9 %collective-permute-start.1 = (bf16[32,1152]{1,0:T(8,128)(2,1)S(1)}, bf16[32,1152]{1,0:T(8,128)(2,1)S(1)}, u32[]{:S(2)}, u32[]{:S(2)}) collective-permute-start(bf16[32,1152]{1,0:T(8,128)(2,1)S(1)} %reshape.95), channel_id=1, source_target_pairs={{0,1},{1,2},{2,3},{3,4},{4,5},{5,6},{6,7},{7,8},{8,9},{9,10},{10,1... | collective-permute-start | bytes 221192 | tf_op jit(solution)/shard_map/ppermute | solution.py:56
  11.8 4.7 %collective-permute-start.3 = (bf16[32,1152]{1,0:T(8,128)(2,1)S(1)}, bf16[32,1152]{1,0:T(8,128)(2,1)S(1)}, u32[]{:S(2)}, u32[]{:S(2)}) collective-permute-start(bf16[32,1152]{1,0:T(8,128)(2,1)S(1)} %reshape.97), channel_id=1, source_target_pairs={{0,63},{1,0},{2,1},{3,2},{4,3},{5,4},{6,5},{7,6},{8,7},{9,8},{10,9... | collective-permute-start | bytes 221192 | tf_op jit(solution)/shard_map/ppermute | solution.py:56
  19.7 18.7 %copy-start.26 = (bf16[8,64,512]{2,1,0:T(8,128)(2,1)S(1)}, bf16[8,64,512]{2,1,0:T(8,128)(2,1)}, u32[]{:S(2)}) copy-start(bf16[8,64,512]{2,1,0:T(8,128)(2,1)} %param.9) | copy-start | bytes 1572868
  19.7 18.8 %copy-start.1 = (bf16[8,64,512]{2,1,0:T(8,128)(2,1)S(1)}, bf16[8,64,512]{2,1,0:T(8,128)(2,1)}, u32[]{:S(2)}) copy-start(bf16[8,64,512]{2,1,0:T(8,128)(2,1)} %own.1) | copy-start | bytes 1572868
  19.7 67.6 %all-to-all-start = ((bf16[64,64,512]{2,1,0:T(8,128)(2,1)}), bf16[64,64,512]{2,1,0:T(8,128)(2,1)}, u32[]{:S(2)}, u32[]{:S(2)}) async-start(bf16[64,64,512]{2,1,0:T(8,128)(2,1)} %broadcast_in_dim.5), calls=%async_computation | async-start | bytes 8388608 | tf_op jit(solution)/shard_map/all_to_all | solution.py:74
  38.3 4.9 %copy-start.10 = (bf16[512,512]{1,0:T(8,128)(2,1)S(1)}, bf16[512,512]{1,0:T(8,128)(2,1)}, u32[]{:S(2)}) copy-start(bf16[512,512]{1,0:T(8,128)(2,1)} %w_out.3) | copy-start | bytes 1572868
  38.3 4.9 %copy-start.11 = (f32[3,512]{1,0:T(4,128)S(1)}, f32[3,512]{1,0:T(4,128)}, u32[]{:S(2)}) copy-start(f32[3,512]{1,0:T(4,128)} %table.1) | copy-start | bytes 18436
  38.3 4.9 %copy-start.12 = (f32[8]{0:T(128)S(1)}, f32[8]{0:T(128)}, u32[]{:S(2)}) copy-start(f32[8]{0:T(128)} %logit.3) | copy-start | bytes 100
  39.1 1.2 copy-start.3
  40.4 25.2 %copy-start.6 = (bf16[216,2048]{1,0:T(8,128)(2,1)}, bf16[216,2048]{1,0:T(8,128)(2,1)S(1)}, u32[]{:S(2)}) copy-start(bf16[216,2048]{1,0:T(8,128)(2,1)S(1)} %get-tuple-element.49.cot) | copy-start | bytes 2654212
  40.4 28.1 %collective-permute-start.7 = (bf16[216,2048]{1,0:T(8,128)(2,1)S(1)}, bf16[216,2048]{1,0:T(8,128)(2,1)S(1)}, u32[]{:S(2)}, u32[]{:S(2)}) collective-permute-start(bf16[216,2048]{1,0:T(8,128)(2,1)S(1)} %get-tuple-element.49.cot), channel_id=1, source_target_pairs={{0,1},{1,0},{2,3},{3,2},{4,5},{5,4},{6,7},{7,6},{8,9},{9,8},{10,11... | collective-permute-start | bytes 2654216 | tf_op jit(solution)/shard_map/ppermute | solution.py:48
  65.6 0.9 copy-start.19
  66.6 0.8 copy-start.22
  67.3 0.9 copy-start.24
  68.2 2.4 %collective-permute-start.6 = (bf16[216,2048]{1,0:T(8,128)(2,1)S(1)}, bf16[216,2048]{1,0:T(8,128)(2,1)S(1)}, u32[]{:S(2)}, u32[]{:S(2)}) collective-permute-start(bf16[216,2048]{1,0:T(8,128)(2,1)S(1)} %get-tuple-element.48.norm.merged_norm), channel_id=1, source_target_pairs={{0,1},{1,0},{2,3},{3,2},{4,5},{5,4},{6,7},{7,6},{8,9},{9,8},{10,11... | collective-permute-start | bytes 2654216 | tf_op jit(solution)/shard_map/ppermute | solution.py:48
  70.7 0.9 copy-start.8
  87.3 1.2 copy-start.7
  88.5 1.2 copy-start.9
  99.1 0.8 copy-start.15
  99.8 0.8 copy-start.17
  100.6 67.8 %all-to-all-start.1 = ((bf16[64,64,512]{2,1,0:T(8,128)(2,1)}), bf16[64,64,512]{2,1,0:T(8,128)(2,1)}, u32[]{:S(2)}, u32[]{:S(2)}) async-start(bf16[64,64,512]{2,1,0:T(8,128)(2,1)} %get-tuple-element.75), calls=%async_computation.1 | async-start | bytes 8388608 | tf_op jit(solution)/shard_map/all_to_all | solution.py:78
  115.3 1.0 copy-start.16
  116.3 1.0 copy-start.18
  117.3 9.9 %copy-start.20 = (bf16[864,512]{1,0:T(8,128)(2,1)S(1)}, bf16[864,512]{1,0:T(8,128)(2,1)}, u32[]{:S(2)}) copy-start(bf16[864,512]{1,0:T(8,128)(2,1)} %copy-done.19) | copy-start | bytes 2654212
  117.3 9.9 %copy-start.25 = (bf16[864,512]{1,0:T(8,128)(2,1)S(1)}, bf16[864,512]{1,0:T(8,128)(2,1)}, u32[]{:S(2)}) copy-start(bf16[864,512]{1,0:T(8,128)(2,1)} %copy-done.24) | copy-start | bytes 2654212
  122.0 0.9 copy-start.5
  123.0 1.2 copy-start.13
  124.2 3.0 %collective-permute-start.9 = (bf16[216,2048]{1,0:T(8,128)(2,1)S(1)}, bf16[216,2048]{1,0:T(8,128)(2,1)S(1)}, u32[]{:S(2)}, u32[]{:S(2)}) collective-permute-start(bf16[216,2048]{1,0:T(8,128)(2,1)S(1)} %get-tuple-element.62), channel_id=1, source_target_pairs={{0,1},{1,0},{2,3},{3,2},{4,5},{5,4},{6,7},{7,6},{8,9},{9,8},{10,11... | collective-permute-start | bytes 2654216 | tf_op jit(solution)/shard_map/ppermute | solution.py:48
  152.7 2.9 %collective-permute-start.10 = (bf16[512,1024]{1,0:T(8,128)(2,1)}, bf16[512,1024]{1,0:T(8,128)(2,1)S(1)}, u32[]{:S(2)}, u32[]{:S(2)}) collective-permute-start(bf16[512,1024]{1,0:T(8,128)(2,1)} %get-tuple-element.74), channel_id=1, source_target_pairs={{0,1},{1,0},{2,3},{3,2},{4,5},{5,4},{6,7},{7,6},{8,9},{9,8},{10,11... | collective-permute-start | bytes 3145736 | tf_op jit(solution)/shard_map/ppermute | solution.py:48
  171.3 11.7 %copy-start.23 = (f32[864,1]{1,0:T(8,128)S(1)}, f32[864,1]{1,0:T(8,128)}, u32[]{:S(2)}) copy-start(f32[864,1]{1,0:T(8,128)} %copy-done.22) | copy-start | bytes 10372
  171.3 24.9 %all-to-all-start.2 = ((bf16[64,8,1024]{2,1,0:T(8,128)(2,1)}), bf16[64,8,1024]{2,1,0:T(8,128)(2,1)}, u32[]{:S(2)}, u32[]{:S(2)}) async-start(bf16[64,8,1024]{2,1,0:T(8,128)(2,1)} %bitcast.7), calls=%async_computation.2 | async-start | bytes 2097152 | tf_op jit(solution)/shard_map/all_to_all | solution.py:78
  180.4 11.4 %collective-permute-start.8 = (bf16[216,2048]{1,0:T(8,128)(2,1)}, bf16[216,2048]{1,0:T(8,128)(2,1)S(1)}, u32[]{:S(2)}, u32[]{:S(2)}) collective-permute-start(bf16[216,2048]{1,0:T(8,128)(2,1)} %copy-done.5), channel_id=1, source_target_pairs={{0,1},{1,0},{2,3},{3,2},{4,5},{5,4},{6,7},{7,6},{8,9},{9,8},{10,11... | collective-permute-start | bytes 2654216 | tf_op jit(solution)/shard_map/ppermute | solution.py:48
  182.9 10.5 %collective-permute-start.12 = (f32[16,512]{1,0:T(8,128)S(1)}, f32[16,512]{1,0:T(8,128)S(1)}, u32[]{:S(2)}, u32[]{:S(2)}) collective-permute-start(f32[16,512]{1,0:T(8,128)S(1)} %get-tuple-element.103), channel_id=1, source_target_pairs={{0,1},{1,0},{2,3},{3,2},{4,5},{5,4},{6,7},{7,6},{8,9},{9,8},{10,11... | collective-permute-start | bytes 98312 | tf_op jit(solution)/shard_map/ppermute | solution.py:48
  182.9 1.4 copy-start.4
  184.3 1.5 copy-start.14
  185.8 1.2 copy-start.21
  187.0 4.8 %copy-start.2 = (f32[216,2048]{1,0:T(8,128)S(1)}, f32[216,2048]{1,0:T(8,128)}, u32[]{:S(2)}) copy-start(f32[216,2048]{1,0:T(8,128)} %get-tuple-element.47.skip) | copy-start | bytes 5308420
  197.5 5.0 %collective-permute-start.11 = (f32[4,1024]{1,0:T(4,128)S(1)}, f32[4,1024]{1,0:T(4,128)S(1)}, u32[]{:S(2)}, u32[]{:S(2)}) collective-permute-start(f32[4,1024]{1,0:T(4,128)S(1)} %get-tuple-element.105), channel_id=1, source_target_pairs={{0,1},{1,0},{2,3},{3,2},{4,5},{5,4},{6,7},{7,6},{8,9},{9,8},{10,11... | collective-permute-start | bytes 49160 | tf_op jit(solution)/shard_map/ppermute | solution.py:48

commit v2 on v1

--- a/solution.py
+++ b/solution.py
@@ -69,13 +69,8 @@
     )
 
 
-def gather(block, axes, count):
-    copies = jnp.broadcast_to(block[None], (count,) + block.shape)
-    return lax.all_to_all(copies, axes, 0, 0, tiled=True)
-
-
-def scatter(blocks, axes):
-    return jnp.sum(lax.all_to_all(blocks, axes, 0, 0, tiled=True).astype(F32), axis=0)
+def add_blocks(blocks):
+    return jnp.sum(blocks.astype(F32), axis=0)
 
 
 def own_rows(block, core):
@@ -89,15 +84,23 @@
     return lax.dot_general(left, right, (((0,), (0,)), ((), ())), preferred_element_type=F32)
 
 
-def rims(field, lat):
-    width = field.shape[-1]
-    near = lax.dynamic_slice_in_dim(field, (1 - lat) * SHIFT, SHIFT, 0)
-    out = [slide(near, 1, 0)]
+def rims(fields, lat, before):
+    def cut(start, cols):
+        part = [field[:, start : start + cols] for field in fields]
+        close = [field.reshape(-1, field.shape[-1]) for field in part]
+        far = [lax.dynamic_slice_in_dim(field, (1 - lat) * SHIFT, SHIFT, 0) for field in part]
+        far = [field.reshape(-1, field.shape[-1]) for field in far]
+        return jnp.concatenate(close, axis=-1), jnp.concatenate(far, axis=-1)
+
+    near = [lax.dynamic_slice_in_dim(field, (1 - lat) * SHIFT, SHIFT, 0) for field in fields]
+    across = slide(jnp.concatenate(near, axis=-1), 1, 0)
+    *fields, before = lax.optimization_barrier((*fields, before))
+    out = [across]
     for step in (1, -1):
-        cut = slice(COLS - SHIFT, COLS) if step == 1 else slice(0, SHIFT)
-        out.append(slide(field[:, cut].reshape(-1, width), 0, step))
-        out.append(slide(near[:, cut].reshape(-1, width), 1, step))
-    return out
+        close, far = cut(COLS - SHIFT if step == 1 else 0, SHIFT)
+        out.append(slide(close, 0, step))
+        out.append(slide(far, 1, step))
+    return out, before
 
 
 def dot(left, right):
@@ -250,6 +253,11 @@
     merged_spread[...] = scale
 
 
+def spread_kernel(block, copies):
+    for chip in range(64):
+        copies[chip] = block[...]
+
+
 def cotangent_kernel(own, across, west, west_far, east, east_far, merged, rounded, wide):
     lay_out(wide, own, across, west, west_far, east, east_far, 4, D + LANES)
     for win, pair, parity, row, cols in chunks(6):
@@ -261,18 +269,25 @@
 
 
 def coarse_kernel(
-    norm, norm_other, cot, cot_other, parts, coarse, grad_pre, split, blocks, merge, sem
+    norm, norm_other, cot, cot_other, parts,
+    coarse_out, grad_out, split, blocks,
+    merge, packed, coarse, grad_pre, sems,
 ):
-    copy = pltpu.make_async_copy(parts, merge, sem)
-    copy.start()
-    copy.wait()
-    w_merge = merge[:, :32, :].reshape(2048, 512)
+    load_merge = pltpu.make_async_copy(parts.at[:, :32], merge, sems.at[0])
+    load_split = pltpu.make_async_copy(parts.at[:, 32:], packed, sems.at[1])
+    store_coarse = pltpu.make_async_copy(coarse, coarse_out, sems.at[2])
+    store_grad = pltpu.make_async_copy(grad_pre, grad_out, sems.at[3])
+    load_split.start()
+    load_merge.start()
+    load_split.wait()
     for j in range(2):
-        pair = merge[:, 32 + 16 * j : 48 + 16 * j, :].astype(F32)
+        pair = packed[:, 16 * j : 16 * j + 16, :].astype(F32)
         for k in range(2):
             quarter = pair[:, 8 * k : 8 * k + 8, :].reshape(512, 512)
             column = (2 * j + k) * 512
             split[:, column : column + 512] = quarter.astype(BF16)
+    load_merge.wait()
+    w_merge = merge[...].reshape(2048, 512)
     slope = 0.7978845608028654
     cubic = 0.044715
     keep = own_mask(CELLS, (ALL_CELLS, 1))
@@ -288,6 +303,8 @@
         grad_pre[i] = grad.astype(BF16)
         own_grads.append((grad * keep).astype(BF16))
         own_cots.append((coarse[i].astype(F32) * keep).astype(BF16))
+    store_coarse.start()
+    store_grad.start()
     for x in range(4):
         chips = slice(x * 16, (x + 1) * 16)
         lanes = slice(x * 512, (x + 1) * 512)
@@ -301,6 +318,8 @@
             quarters.append(block.reshape(64, 8, 512))
         pair = jnp.concatenate(quarters, axis=1).astype(BF16)
         blocks[:, 32 + 16 * j : 48 + 16 * j, :] = pair
+    store_coarse.wait()
+    store_grad.wait()
 
 
 def partial_kernel(
@@ -421,7 +440,7 @@
 
 
 def kernel_call(
-    kernel, name, outs, scratch, args, scalars=0, ahead=0, in_place=0, flops=0, moved=0, curves=0
+    kernel, name, outs, scratch, args, scalars=0, ahead=0, in_place=0, far_outs=0, flops=0, moved=0
 ):
     count = len(args)
     specs = []
@@ -437,10 +456,13 @@
         kernel,
         out_shape=shapes,
         in_specs=specs,
-        out_specs=[pl.BlockSpec(memory_space=pltpu.VMEM)] * len(outs),
+        out_specs=[
+            pl.BlockSpec(memory_space=pl.ANY if index < far_outs else pltpu.VMEM)
+            for index in range(len(outs))
+        ],
         scratch_shapes=scratch,
         compiler_params=pltpu.CompilerParams(vmem_limit_bytes=VMEM_BYTES),
-        cost_estimate=pl.CostEstimate(flops=flops, bytes_accessed=moved, transcendentals=curves),
+        cost_estimate=pl.CostEstimate(flops=flops, bytes_accessed=moved, transcendentals=0),
         name=name,
     )(*args)
 
@@ -453,18 +475,21 @@
     spot = jnp.stack([lat, core]).astype(jnp.int32)
     kinds = jnp.broadcast_to(surface.astype(BF16)[:, :, None], (ROWS, COLS, LANES))
     own_fields = jnp.concatenate([fields, kinds], axis=-1)
-    rim = rims(jnp.concatenate([own_fields, cotangent], axis=-1), lat)
 
     index = jnp.arange(1024, dtype=jnp.int32)
     source = index % 512 // 8 * 16 + index // 512 * 8 + index % 8
     runs = (index[:, None] == source[None, :]).astype(BF16)
     sorted_merge = jnp.dot(w_merge, runs, preferred_element_type=F32).astype(BF16)
     far = move(half_of(sorted_merge, 1 - core), c=1)
+    rim, far = rims((fields, kinds, cotangent), lat, far)
     merge_block = join_cores(half_of(sorted_merge, core), far, core, 0)
     split_block = w_split.reshape(8, 4, 512).transpose(1, 0, 2).reshape(32, 512)
     block = jnp.concatenate([merge_block, split_block], axis=0)
-    *rim, block = lax.optimization_barrier((*rim, block))
-    mine = gather(block, CHIP_AXES, 64)
+    (copies,) = kernel_call(
+        spread_kernel, "spread_weights", [((64, 64, 512), BF16)], [], (block,), moved=4_000_000
+    )
+    *rim, copies = lax.optimization_barrier((*rim, copies))
+    mine = lax.all_to_all(copies, CHIP_AXES, 0, 0, tiled=True)
 
     cells = (ALL_CELLS, 4 * D)
     skip, merged_norm, merged_spread, normed, spread, units, unit_scale, weights, attended = kernel_call(
@@ -496,7 +521,7 @@
         moved=8_000_000,
     )
     norm_other, cot_other = move(merged_norm, c=1), move(cot_rounded, c=1)
-    norm_other, cot_other, mine = lax.optimization_barrier((norm_other, cot_other, mine))
+    merged_spread, mine = lax.optimization_barrier((merged_spread, mine))
     coarse, grad_pre, split, blocks = kernel_call(
         coarse_kernel,
         "coarse",
@@ -506,14 +531,21 @@
             ((512, 2048), BF16),
             ((64, 64, 512), BF16),
         ],
-        [pltpu.VMEM((64, 64, 512), BF16), pltpu.SemaphoreType.DMA],
+        [
+            pltpu.VMEM((64, 32, 512), BF16),
+            pltpu.VMEM((64, 32, 512), BF16),
+            pltpu.VMEM((2, ALL_CELLS, 512), BF16),
+            pltpu.VMEM((2, ALL_CELLS, 512), BF16),
+            pltpu.SemaphoreType.DMA((4,)),
+        ],
         (merged_norm, norm_other, cot_rounded, cot_other, mine),
         in_place=1,
+        far_outs=2,
         flops=8_000_000_000,
         moved=15_000_000,
     )
     split, blocks = lax.optimization_barrier((split, blocks))
-    blocks = scatter(blocks, CHIP_AXES)
+    blocks = lax.all_to_all(blocks, CHIP_AXES, 0, 0, tiled=True)
     grad_mine, grad_other, out_mine, out_other = kernel_call(
         partial_kernel,
         "partial_products",
@@ -571,14 +603,19 @@
     )
     fine_half = (fine_mine.astype(F32) + move(fine_other, c=1).astype(F32)).astype(BF16)
     fine_half, blocks = lax.optimization_barrier((fine_half, blocks))
-    fine_grads = own_rows(scatter(fine_half.reshape(64, D // 64, 1024), CHIP_AXES), core)
+    fine_blocks = lax.all_to_all(fine_half.reshape(64, D // 64, 1024), CHIP_AXES, 0, 0, tiled=True)
+    fine_sum = add_blocks(fine_blocks)
+    fine_own = lax.dynamic_slice_in_dim(fine_sum, core * 4, 4, 0)
+    fine_far = move(lax.dynamic_slice_in_dim(fine_sum, (1 - core) * 4, 4, 0), c=1)
+    first, second = jnp.where(core == 0, fine_own, fine_far), jnp.where(core == 0, fine_far, fine_own)
+    blocks = add_blocks(blocks)
     grad_split = blocks[32:].reshape(4, 8, 512).transpose(1, 0, 2).reshape(8, 2048)
     grad_merge = own_rows(blocks[:32], core).reshape(16, 2, 64, 8).transpose(0, 2, 1, 3)
     return (
         decoded,
         grad_fields,
-        fine_grads[:, : 3 * D],
-        fine_grads[:, 3 * D :],
+        jnp.concatenate([first, second[:, :D]], axis=1),
+        second[:, D:],
         grad_merge.reshape(16, 1024),
         grad_split,
     )

time: 205 us -> 197 us (0.961)
  local copies, waits for them, and re-layouts: 23.9 us -> 15.8 us
  starting transfers between devices: 63.6 us -> 58.1 us
  Pallas kernels: 68.7 us -> 72 us
  waiting for transfers between devices: 37.9 us -> 41.1 us
    all_to_all x3, starting transfers between devices: 42.4 us -> 36 us  [the longest x1 14.2 us: per_device(): blocks = lax.all_to_all(blocks, CHIP_AXES, 0, 0, tiled=True)]
    unnamed x57, local copies, waits for them, and re-layouts: 18.4 us -> 12.1 us
    ppermute x5, waiting for transfers between devices: 1.51 us -> 5.14 us  [slide(): return lax.ppermute(value, AXES, pairs)]
    pallas_call x7 -> x8, Pallas kernels: 68.7 us -> 72 us  [kernel_call(): pl.pallas_call(kernel, out_shape=shapes, in_specs=specs, out_specs=[pl.Bl...]
    broadcast_in_dim x1 -> x0, local copies, waits for them, and re-layouts: 2.49 us -> none  [gather(): copies = jnp.broadcast_to(block[None], (count,) + block.shape)]
    ppermute x8, waiting for transfers between devices: 6.68 us -> 4.57 us  [move(): return lax.ppermute(value, AXES, pairs)]
  transfers between devices with their start and end apart: 16 -> 16, of which waited for: 9 -> 7; matrix products, arithmetic and copies ran while one was open for 3% -> 5% of each run, Pallas kernels for 29% -> 31%
where the time goes in v2:
time: 197 us; the launch traced here: 196 us
  Pallas kernels  72 us (37%)
  starting transfers between devices  58.1 us (29%)
  waiting for transfers between devices  41.1 us (21%)
  local copies, waits for them, and re-layouts  15.8 us (8%)
  other arithmetic  7.36 us (4%)
    pallas_call x8, Pallas kernels, kernel_call(): pl.pallas_call(kernel, out_shape=shapes, in_specs=specs, out_specs=[pl.Bl...  72 us
    all_to_all x1, waiting for transfers between devices, per_device(): mine = lax.all_to_all(copies, CHIP_AXES, 0, 0, tiled=True)  19.5 us
    all_to_all x1, starting transfers between devices, per_device(): blocks = lax.all_to_all(blocks, CHIP_AXES, 0, 0, tiled=True)  14.2 us
    ppermute x8, starting transfers between devices, move(): return lax.ppermute(value, AXES, pairs)  12.3 us
    unnamed x57, local copies, waits for them, and re-layouts  12.1 us
    all_to_all x1, starting transfers between devices, per_device(): mine = lax.all_to_all(copies, CHIP_AXES, 0, 0, tiled=True)  11.7 us
    all_to_all x1, waiting for transfers between devices, per_device(): blocks = lax.all_to_all(blocks, CHIP_AXES, 0, 0, tiled=True)  10.6 us
    all_to_all x1, starting transfers between devices, per_device(): lax.all_to_all(fine_half.reshape(64, D // 64, 1024), CHIP_AXES, 0, 0, til...  10.2 us
  transfers between devices with their start and end apart: 16, of which 7 were waited for; matrix products, arithmetic and copies ran while one was open for 5% of the time, Pallas kernels for 31%

profile of v2, /device:TPU:1, one launch (start us, length us, event | category | flops | bytes accessed | tf_op | source)
XLA Modules:
  0.0 196.3 jit_solution(1419658420325909273)
XLA Ops:
  0.7 0.7 copy-done
  1.4 0.7 fusion.2
  2.2 1.5 collective-permute-start.1
  3.7 0.7 convert_element_type.23
  4.4 1.1 constant_dynamic-slice_fusion.9
  5.4 0.1 broadcast_in_dim.5
  5.5 0.1 pad_maximum_fusion.1
  5.6 1.4 collective-permute-start
  7.0 0.1 broadcast_in_dim.4
  7.1 0.1 fusion.25
  7.5 1.5 collective-permute-start.3
  9.0 0.4 collective-permute-start.5
  9.4 2.4 %collective-permute-start.2 = (bf16[32,1152]{1,0:T(8,128)(2,1)S(1)}, bf16[32,1152]{1,0:T(8,128)(2,1)S(1)}, u32[]{:S(2)}, u32[]{:S(2)}) collective-permute-start(bf16[32,1152]{1,0:T(8,128)(2,1)S(1)} %pad_maximum_fusion.2), channel_id=1, source_target_pairs={{0,1},{1,2},{2,3},{3,4},{4,5},{5,6},{6,7},{7,8},{8,9},{9,10},{10,1... | collective-permute-start | bytes 221192 | tf_op jit(solution)/shard_map/ppermute | solution.py:56
  11.9 4.1 %collective-permute-start.4 = (bf16[32,1152]{1,0:T(8,128)(2,1)S(1)}, bf16[32,1152]{1,0:T(8,128)(2,1)S(1)}, u32[]{:S(2)}, u32[]{:S(2)}) collective-permute-start(bf16[32,1152]{1,0:T(8,128)(2,1)S(1)} %pad_maximum_fusion.3), channel_id=1, source_target_pairs={{0,63},{1,0},{2,1},{3,2},{4,3},{5,4},{6,5},{7,6},{8,7},{9,8},{10,9... | collective-permute-start | bytes 221192 | tf_op jit(solution)/shard_map/ppermute | solution.py:56
  16.0 0.3 spread_weights.1
  16.3 2.0 %copy-done.1 = bf16[64,64,512]{2,1,0:T(8,128)(2,1)} copy-done((bf16[64,64,512]{2,1,0:T(8,128)(2,1)}, bf16[64,64,512]{2,1,0:T(8,128)(2,1)S(1)}, u32[]{:S(2)}) %copy-start.1) | copy-done | bytes 4194328
  18.3 3.9 %collective-permute-done.3.west_far = bf16[16,1152]{1,0:T(8,128)(2,1)S(1)} collective-permute-done((bf16[16,1152]{1,0:T(8,128)(2,1)S(1)}, bf16[16,1152]{1,0:T(8,128)(2,1)S(1)}, u32[]{:S(2)}, u32[]{:S(2)}) %collective-permute-start.3) | collective-permute-done | bytes 36896 | tf_op jit(solution)/shard_map/ppermute | solution.py:56
  22.2 1.2 collective-permute-done.5.east_far
  23.4 11.7 %all-to-all-start = ((bf16[64,64,512]{2,1,0:T(8,128)(2,1)}), bf16[64,64,512]{2,1,0:T(8,128)(2,1)}, u32[]{:S(2)}, u32[]{:S(2)}) async-start(bf16[64,64,512]{2,1,0:T(8,128)(2,1)} %copy-done.1), calls=%async_computation | async-start | bytes 8388608 | tf_op jit(solution)/shard_map/all_to_all | solution.py:492
  35.1 0.1 pad_add_fusion.spot
  35.2 0.1 pad_maximum_fusion.own
  35.3 0.6 cotangent_cells.1
  35.9 1.2 copy-done.4
  37.2 2.2 %collective-permute-start.7 = (bf16[216,2048]{1,0:T(8,128)(2,1)S(1)}, bf16[216,2048]{1,0:T(8,128)(2,1)}, u32[]{:S(2)}, u32[]{:S(2)}) collective-permute-start(bf16[216,2048]{1,0:T(8,128)(2,1)S(1)} %get-tuple-element.59.cot), channel_id=1, source_target_pairs={{0,1},{1,0},{2,3},{3,2},{4,5},{5,4},{6,7},{7,6},{8,9},{9,8},{10,11... | collective-permute-start | bytes 2654216 | tf_op jit(solution)/shard_map/ppermute | solution.py:48
  39.4 22.3 %fine_forward.1 = (f32[216,2048]{1,0:T(8,128)}, bf16[216,2048]{1,0:T(8,128)(2,1)S(1)}, f32[216,1]{1,0:T(8,128)S(1)}, bf16[864,512]{1,0:T(8,128)(2,1)S(1)}, f32[8...) custom-call(s32[2]{0:T(128)S(1)} %pad_add_fusion.spot, ...), custom_call_target="tpu_custom_call" | custom-call | flops 15000000512 | bytes 12000000 | tf_op jit(solution)/shard_map/fine_forward/pallas_call | solution.py:455
  61.7 0.9 copy-done.19
  62.6 0.8 copy-done.22
  63.4 0.9 copy-done.24
  64.3 0.0 collective-permute-start.6
  64.3 19.5 %all-to-all-done.parts = bf16[64,64,512]{2,1,0:T(8,128)(2,1)} async-done(((bf16[64,64,512]{2,1,0:T(8,128)(2,1)}), bf16[64,64,512]{2,1,0:T(8,128)(2,1)}, u32[]{:S(2)}, u32[]{:S(2)}) %all-to-all-start) | async-done | bytes 4194336 | tf_op jit(solution)/shard_map/all_to_all | solution.py:492
  83.8 11.6 %coarse.1 = (bf16[2,216,512]{2,1,0:T(8,128)(2,1)S(1)}, bf16[2,216,512]{2,1,0:T(8,128)(2,1)S(1)}, bf16[512,2048]{1,0:T(8,128)(2,1)}, bf16[64,64,512]{2,1,0:T(8,128)(2,1)}) custom-call(bf16[216,2048]{1,0:T(8,128)(2,1)S(1)} %get-tuple-element.58.norm.merged_norm, bf16[216,2048]{1,0:T(8,128)(2,1)S(1)} %collective-permute-done.6.norm_other, ...), custom_call_target="tpu_custom_call" | custom-call | flops 8000000000 | bytes 15000000 | tf_op jit(solution)/shard_map/coarse/pallas_call | solution.py:455
  95.4 0.8 copy-done.15
  96.2 0.8 copy-done.17
  96.9 14.2 %all-to-all-start.1 = ((bf16[64,64,512]{2,1,0:T(8,128)(2,1)}), bf16[64,64,512]{2,1,0:T(8,128)(2,1)}, u32[]{:S(2)}, u32[]{:S(2)}) async-start(bf16[64,64,512]{2,1,0:T(8,128)(2,1)} %get-tuple-element.81), calls=%async_computation.1 | async-start | bytes 8388608 | tf_op jit(solution)/shard_map/all_to_all | solution.py:548
  111.2 1.0 copy-done.18
  112.2 4.7 %partial_products.1 = (f32[216,2048]{1,0:T(8,128)S(1)}, bf16[216,2048]{1,0:T(8,128)(2,1)S(1)}, f32[216,2048]{1,0:T(8,128)S(1)}, bf16[216,2048]{1,0:T(8,128)(2,1)S(1)}) custom-call(bf16[64,64,512]{2,1,0:T(8,128)(2,1)} %all-to-all-done.parts, bf16[2,216,512]{2,1,0:T(8,128)(2,1)S(1)} %copy-done.16, bf16[2,216,512]{2,1,0:T(8,128)(2,1)S(1)} %copy-done.18, ...), custom_call_target="tpu_custom_call" | custom-call | flops 3000000000 | bytes 10000000 | tf_op jit(solution)/shard_map/partial_products/pallas_call | solution.py:455
  116.9 1.0 copy-done.6
  117.9 1.2 copy-done.13
  119.1 1.2 collective-permute-start.9
  120.4 2.1 %collective-permute-done.9.received = bf16[216,2048]{1,0:T(8,128)(2,1)S(1)} collective-permute-done((bf16[216,2048]{1,0:T(8,128)(2,1)S(1)}, bf16[216,2048]{1,0:T(8,128)(2,1)S(1)}, u32[]{:S(2)}, u32[]{:S(2)}) %collective-permute-start.9) | collective-permute-done | bytes 884768 | tf_op jit(solution)/shard_map/ppermute | solution.py:48
  122.4 25.2 %fine_backward.1 = (f32[216,2048]{1,0:T(8,128)}, bf16[864,1536]{1,0:T(8,128)(2,1)}, bf16[512,1024]{1,0:T(8,128)(2,1)S(1)}, bf16[512,1024]{1,0:T(8,128)(2,1)}) custom-call(s32[2]{0:T(128)S(1)} %pad_add_fusion.spot, f32[8]{0:T(128)S(1)} %copy-done.12, f32[216,2048]{1,0:T(8,128)} %copy-done.13, bf16[216,2048]{1,0:T(8,128)(2,1)S(1)} %collective-permute-done.9.received, ...), custom_call_target="tpu_custom_call" | custom-call | flops 15000000512 | bytes 15000000 | tf_op jit(solution)/shard_map/fine_backward/pallas_call | solution.py:455
  147.6 0.4 collective-permute-start.10
  148.0 0.1 collective-permute-start.8
  148.1 2.5 %collective-permute-done.10 = bf16[512,1024]{1,0:T(8,128)(2,1)} collective-permute-done((bf16[512,1024]{1,0:T(8,128)(2,1)}, bf16[512,1024]{1,0:T(8,128)(2,1)}, u32[]{:S(2)}, u32[]{:S(2)}) %collective-permute-start.10) | collective-permute-done | bytes 1048608 | tf_op jit(solution)/shard_map/ppermute | solution.py:48
  150.6 2.6 %add_convert_fusion = bf16[512,1024]{1,0:T(8,128)(2,1)} fusion(bf16[512,1024]{1,0:T(8,128)(2,1)} %collective-permute-done.10, bf16[512,1024]{1,0:T(8,128)(2,1)S(1)} %get-tuple-element.79), kind=kLoop, calls=%fused_computation.4 | loop fusion | flops 2097152 | bytes 3145728 | tf_op jit(solution)/shard_map/convert_element_type | solution.py:604
  153.2 10.6 %all-to-all-done.1 = bf16[64,64,512]{2,1,0:T(8,128)(2,1)} async-done(((bf16[64,64,512]{2,1,0:T(8,128)(2,1)}), bf16[64,64,512]{2,1,0:T(8,128)(2,1)}, u32[]{:S(2)}, u32[]{:S(2)}) %all-to-all-start.1) | async-done | bytes 4194336 | tf_op jit(solution)/shard_map/all_to_all | solution.py:548
  163.8 10.2 %all-to-all-start.2 = ((bf16[64,8,1024]{2,1,0:T(8,128)(2,1)}), bf16[64,8,1024]{2,1,0:T(8,128)(2,1)S(1)}, u32[]{:S(2)}, u32[]{:S(2)}) async-start(bf16[64,8,1024]{2,1,0:T(8,128)(2,1)} %bitcast.27), calls=%async_computation.2 | async-start | bytes 2097152 | tf_op jit(solution)/shard_map/all_to_all | solution.py:606
  174.1 3.0 %convert_reduce_fusion = f32[64,512]{1,0:T(8,128)S(1)} fusion(bf16[64,64,512]{2,1,0:T(8,128)(2,1)} %all-to-all-done.1), kind=kLoop, calls=%fused_computation | loop fusion | flops 4161536 | bytes 4325376 | tf_op jit(solution)/shard_map/reduce_sum | solution.py:73
  177.1 0.6 fusion.27
  177.7 2.3 %collective-permute-start.12 = (f32[16,512]{1,0:T(8,128)S(1)}, f32[16,512]{1,0:T(8,128)S(1)}, u32[]{:S(2)}, u32[]{:S(2)}) collective-permute-start(f32[16,512]{1,0:T(8,128)S(1)} %get-tuple-element.111), channel_id=1, source_target_pairs={{0,1},{1,0},{2,3},{3,2},{4,5},{5,4},{6,7},{7,6},{8,9},{9,8},{10,11... | collective-permute-start | bytes 98312 | tf_op jit(solution)/shard_map/ppermute | solution.py:48
  180.0 4.7 %field_grad.1 = bf16[8,64,512]{2,1,0:T(8,128)(2,1)} custom-call(f32[216,2048]{1,0:T(8,128)S(1)} %copy-done.14, bf16[864,1536]{1,0:T(8,128)(2,1)} %get-tuple-element.77.grad_packed, bf16[864,512]{1,0:T(8,128)(2,1)S(1)} %copy-done.21, f32[864,1]{1,0:T(8,128)S(1)} %copy-done.23, bf16[512,1536]{1,0:T(8,128)(2,1)S(1)} %copy-done.5), custom_call_target="tpu_custom_call" | custom-call | flops 4000000000 | bytes 8000000 | tf_op jit(solution)/shard_map/field_grad/pallas_call | solution.py:455
  184.8 2.5 %decode.1 = bf16[8,64,512]{2,1,0:T(8,128)(2,1)} custom-call(f32[216,2048]{1,0:T(8,128)S(1)} %copy-done.2, f32[216,2048]{1,0:T(8,128)S(1)} %get-tuple-element.65.out_mine, bf16[216,2048]{1,0:T(8,128)(2,1)} %collective-permute-done.8.received), custom_call_target="tpu_custom_call" | custom-call | bytes 8000000 | tf_op jit(solution)/shard_map/decode/pallas_call | solution.py:455
  187.3 0.1 copy.22
  187.4 0.1 copy.24
  187.6 0.0 collective-permute-done.12
  187.6 0.1 copy.23
  187.7 0.1 copy.25
  187.9 1.4 all-to-all-done.2
  189.2 0.2 convert_reduce_fusion.1
  189.4 4.5 %collective-permute-start.11 = (f32[4,1024]{1,0:T(4,128)S(1)}, f32[4,1024]{1,0:T(4,128)S(1)}, u32[]{:S(2)}, u32[]{:S(2)}) collective-permute-start(f32[4,1024]{1,0:T(4,128)S(1)} %constant_dynamic-slice_fusion.2), channel_id=1, source_target_pairs={{0,1},{1,0},{2,3},{3,2},{4,5},{5,4},{6,7},{7,6},{8,9},{9,8},{10,11... | collective-permute-start | bytes 49160 | tf_op jit(solution)/shard_map/ppermute | solution.py:48
  194.0 0.3 copy.28
  194.3 0.8 copy.29
  195.1 0.6 fusion.29
  195.7 0.6 pad_maximum_fusion.7
  (80 shorter events, 0.4 us)
Async XLA Ops:
  0.6 0.8 copy-start
  0.6 6.5 %copy-start.3 = (bf16[8,64,512]{2,1,0:T(8,128)(2,1)S(1)}, bf16[8,64,512]{2,1,0:T(8,128)(2,1)}, u32[]{:S(2)}) copy-start(bf16[8,64,512]{2,1,0:T(8,128)(2,1)} %own.1) | copy-start | bytes 1572868
  0.7 6.5 %copy-start.26 = (bf16[8,64,512]{2,1,0:T(8,128)(2,1)S(1)}, bf16[8,64,512]{2,1,0:T(8,128)(2,1)}, u32[]{:S(2)}) copy-start(bf16[8,64,512]{2,1,0:T(8,128)(2,1)} %param.9) | copy-start | bytes 1572868
  2.1 13.8 %copy-start.27 = (bf16[8,2048]{1,0:T(8,128)(2,1)S(1)}, bf16[8,2048]{1,0:T(8,128)(2,1)}, u32[]{:S(2)}) copy-start(bf16[8,2048]{1,0:T(8,128)(2,1)} %param.16) | copy-start | bytes 98308
  2.2 4.8 %collective-permute-start.1 = (bf16[16,512]{1,0:T(8,128)(2,1)S(1)}, bf16[16,512]{1,0:T(8,128)(2,1)S(1)}, u32[]{:S(2)}, u32[]{:S(2)}) collective-permute-start(bf16[16,512]{1,0:T(8,128)(2,1)S(1)} %get-tuple-element.115), channel_id=1, source_target_pairs={{0,1},{1,0},{2,3},{3,2},{4,5},{5,4},{6,7},{7,6},{8,9},{9,8},{10,11... | collective-permute-start | bytes 49160 | tf_op jit(solution)/shard_map/ppermute | solution.py:48
  5.6 17.8 %collective-permute-start = (bf16[4,64,1152]{2,1,0:T(8,128)(2,1)S(1)}, bf16[4,64,1152]{2,1,0:T(8,128)(2,1)S(1)}, u32[]{:S(2)}, u32[]{:S(2)}) collective-permute-start(bf16[4,64,1152]{2,1,0:T(8,128)(2,1)S(1)} %pad_maximum_fusion.1), channel_id=1, source_target_pairs={{0,64},{1,65},{2,66},{3,67},{4,68},{5,69},{6,70},{7,71},{8,72},{9,... | collective-permute-start | bytes 1769480 | tf_op jit(solution)/shard_map/ppermute | solution.py:56
  7.5 14.7 %collective-permute-start.3 = (bf16[16,1152]{1,0:T(8,128)(2,1)S(1)}, bf16[16,1152]{1,0:T(8,128)(2,1)S(1)}, u32[]{:S(2)}, u32[]{:S(2)}) collective-permute-start(bf16[16,1152]{1,0:T(8,128)(2,1)S(1)} %pad_maximum_fusion.5), channel_id=1, source_target_pairs={{0,65},{1,66},{2,67},{3,68},{4,69},{5,70},{6,71},{7,72},{8,73},{9,... | collective-permute-start | bytes 110600 | tf_op jit(solution)/shard_map/ppermute | solution.py:56
  9.0 14.4 %collective-permute-start.5 = (bf16[16,1152]{1,0:T(8,128)(2,1)S(1)}, bf16[16,1152]{1,0:T(8,128)(2,1)S(1)}, u32[]{:S(2)}, u32[]{:S(2)}) collective-permute-start(bf16[16,1152]{1,0:T(8,128)(2,1)S(1)} %pad_maximum_fusion.6), channel_id=1, source_target_pairs={{0,127},{1,64},{2,65},{3,66},{4,67},{5,68},{6,69},{7,70},{8,71},{9... | collective-permute-start | bytes 110600 | tf_op jit(solution)/shard_map/ppermute | solution.py:56
  9.4 14.0 %collective-permute-start.2 = (bf16[32,1152]{1,0:T(8,128)(2,1)S(1)}, bf16[32,1152]{1,0:T(8,128)(2,1)S(1)}, u32[]{:S(2)}, u32[]{:S(2)}) collective-permute-start(bf16[32,1152]{1,0:T(8,128)(2,1)S(1)} %pad_maximum_fusion.2), channel_id=1, source_target_pairs={{0,1},{1,2},{2,3},{3,4},{4,5},{5,6},{6,7},{7,8},{8,9},{9,10},{10,1... | collective-permute-start | bytes 221192 | tf_op jit(solution)/shard_map/ppermute | solution.py:56
  11.9 11.6 %collective-permute-start.4 = (bf16[32,1152]{1,0:T(8,128)(2,1)S(1)}, bf16[32,1152]{1,0:T(8,128)(2,1)S(1)}, u32[]{:S(2)}, u32[]{:S(2)}) collective-permute-start(bf16[32,1152]{1,0:T(8,128)(2,1)S(1)} %pad_maximum_fusion.3), channel_id=1, source_target_pairs={{0,63},{1,0},{2,1},{3,2},{4,3},{5,4},{6,5},{7,6},{8,7},{9,8},{10,9... | collective-permute-start | bytes 221192 | tf_op jit(solution)/shard_map/ppermute | solution.py:56
  16.3 2.0 %copy-start.1 = (bf16[64,64,512]{2,1,0:T(8,128)(2,1)}, bf16[64,64,512]{2,1,0:T(8,128)(2,1)S(1)}, u32[]{:S(2)}) copy-start(bf16[64,64,512]{2,1,0:T(8,128)(2,1)S(1)} %spread_weights.1) | copy-start | bytes 12582916
  23.4 60.4 %all-to-all-start = ((bf16[64,64,512]{2,1,0:T(8,128)(2,1)}), bf16[64,64,512]{2,1,0:T(8,128)(2,1)}, u32[]{:S(2)}, u32[]{:S(2)}) async-start(bf16[64,64,512]{2,1,0:T(8,128)(2,1)} %copy-done.1), calls=%async_computation | async-start | bytes 8388608 | tf_op jit(solution)/shard_map/all_to_all | solution.py:492
  35.1 4.3 %copy-start.9 = (bf16[512,512]{1,0:T(8,128)(2,1)S(1)}, bf16[512,512]{1,0:T(8,128)(2,1)}, u32[]{:S(2)}) copy-start(bf16[512,512]{1,0:T(8,128)(2,1)} %w_out.3) | copy-start | bytes 1572868
  35.1 4.3 %copy-start.11 = (f32[3,512]{1,0:T(4,128)S(1)}, f32[3,512]{1,0:T(4,128)}, u32[]{:S(2)}) copy-start(f32[3,512]{1,0:T(4,128)} %table.1) | copy-start | bytes 18436
  35.1 4.2 %copy-start.12 = (f32[8]{0:T(128)S(1)}, f32[8]{0:T(128)}, u32[]{:S(2)}) copy-start(f32[8]{0:T(128)} %logit.3) | copy-start | bytes 100
  35.9 1.2 copy-start.4
  37.2 46.7 %collective-permute-start.7 = (bf16[216,2048]{1,0:T(8,128)(2,1)S(1)}, bf16[216,2048]{1,0:T(8,128)(2,1)}, u32[]{:S(2)}, u32[]{:S(2)}) collective-permute-start(bf16[216,2048]{1,0:T(8,128)(2,1)S(1)} %get-tuple-element.59.cot), channel_id=1, source_target_pairs={{0,1},{1,0},{2,3},{3,2},{4,5},{5,4},{6,7},{7,6},{8,9},{9,8},{10,11... | collective-permute-start | bytes 2654216 | tf_op jit(solution)/shard_map/ppermute | solution.py:48
  61.7 0.9 copy-start.19
  62.6 0.8 copy-start.22
  63.4 0.9 copy-start.24
  64.3 31.1 %copy-start.7 = (bf16[216,2048]{1,0:T(8,128)(2,1)}, bf16[216,2048]{1,0:T(8,128)(2,1)S(1)}, u32[]{:S(2)}) copy-start(bf16[216,2048]{1,0:T(8,128)(2,1)S(1)} %get-tuple-element.58.norm.merged_norm) | copy-start | bytes 2654212
  64.3 19.5 %collective-permute-start.6 = (bf16[216,2048]{1,0:T(8,128)(2,1)S(1)}, bf16[216,2048]{1,0:T(8,128)(2,1)S(1)}, u32[]{:S(2)}, u32[]{:S(2)}) collective-permute-start(bf16[216,2048]{1,0:T(8,128)(2,1)S(1)} %get-tuple-element.58.norm.merged_norm), channel_id=1, source_target_pairs={{0,1},{1,0},{2,3},{3,2},{4,5},{5,4},{6,7},{7,6},{8,9},{9,8},{10,11... | collective-permute-start | bytes 2654216 | tf_op jit(solution)/shard_map/ppermute | solution.py:48
  95.4 0.8 copy-start.15
  96.2 0.8 copy-start.17
  96.2 15.0 %copy-start.16 = (bf16[2,216,512]{2,1,0:T(8,128)(2,1)S(1)}, bf16[2,216,512]{2,1,0:T(8,128)(2,1)}, u32[]{:S(2)}) copy-start(bf16[2,216,512]{2,1,0:T(8,128)(2,1)} %copy-done.15) | copy-start | bytes 1327108
  96.9 66.9 %all-to-all-start.1 = ((bf16[64,64,512]{2,1,0:T(8,128)(2,1)}), bf16[64,64,512]{2,1,0:T(8,128)(2,1)}, u32[]{:S(2)}, u32[]{:S(2)}) async-start(bf16[64,64,512]{2,1,0:T(8,128)(2,1)} %get-tuple-element.81), calls=%async_computation.1 | async-start | bytes 8388608 | tf_op jit(solution)/shard_map/all_to_all | solution.py:548
  111.1 1.0 copy-start.18
  112.2 10.2 %copy-start.8 = (bf16[216,2048]{1,0:T(8,128)(2,1)S(1)}, bf16[216,2048]{1,0:T(8,128)(2,1)}, u32[]{:S(2)}) copy-start(bf16[216,2048]{1,0:T(8,128)(2,1)} %copy-done.7) | copy-start | bytes 2654212
  112.2 10.2 %copy-start.10 = (bf16[512,512]{1,0:T(8,128)(2,1)S(1)}, bf16[512,512]{1,0:T(8,128)(2,1)}, u32[]{:S(2)}) copy-start(bf16[512,512]{1,0:T(8,128)(2,1)} %w_out.3) | copy-start | bytes 1572868
  112.2 10.2 %copy-start.20 = (bf16[864,512]{1,0:T(8,128)(2,1)S(1)}, bf16[864,512]{1,0:T(8,128)(2,1)}, u32[]{:S(2)}) copy-start(bf16[864,512]{1,0:T(8,128)(2,1)} %copy-done.19) | copy-start | bytes 2654212
  112.2 10.2 %copy-start.25 = (bf16[864,512]{1,0:T(8,128)(2,1)S(1)}, bf16[864,512]{1,0:T(8,128)(2,1)}, u32[]{:S(2)}) copy-start(bf16[864,512]{1,0:T(8,128)(2,1)} %copy-done.24) | copy-start | bytes 2654212
  116.9 1.0 copy-start.6
  117.9 1.2 copy-start.13
  119.1 3.3 %collective-permute-start.9 = (bf16[216,2048]{1,0:T(8,128)(2,1)S(1)}, bf16[216,2048]{1,0:T(8,128)(2,1)S(1)}, u32[]{:S(2)}, u32[]{:S(2)}) collective-permute-start(bf16[216,2048]{1,0:T(8,128)(2,1)S(1)} %get-tuple-element.68), channel_id=1, source_target_pairs={{0,1},{1,0},{2,3},{3,2},{4,5},{5,4},{6,7},{7,6},{8,9},{9,8},{10,11... | collective-permute-start | bytes 2654216 | tf_op jit(solution)/shard_map/ppermute | solution.py:48
  147.6 3.0 %collective-permute-start.10 = (bf16[512,1024]{1,0:T(8,128)(2,1)}, bf16[512,1024]{1,0:T(8,128)(2,1)}, u32[]{:S(2)}, u32[]{:S(2)}) collective-permute-start(bf16[512,1024]{1,0:T(8,128)(2,1)} %get-tuple-element.80), channel_id=1, source_target_pairs={{0,1},{1,0},{2,3},{3,2},{4,5},{5,4},{6,7},{7,6},{8,9},{9,8},{10,11... | collective-permute-start | bytes 3145736 | tf_op jit(solution)/shard_map/ppermute | solution.py:48
  148.0 36.8 %collective-permute-start.8 = (bf16[216,2048]{1,0:T(8,128)(2,1)}, bf16[216,2048]{1,0:T(8,128)(2,1)}, u32[]{:S(2)}, u32[]{:S(2)}) collective-permute-start(bf16[216,2048]{1,0:T(8,128)(2,1)} %copy-done.6), channel_id=1, source_target_pairs={{0,1},{1,0},{2,3},{3,2},{4,5},{5,4},{6,7},{7,6},{8,9},{9,8},{10,11... | collective-permute-start | bytes 2654216 | tf_op jit(solution)/shard_map/ppermute | solution.py:48
  163.8 25.4 %all-to-all-start.2 = ((bf16[64,8,1024]{2,1,0:T(8,128)(2,1)}), bf16[64,8,1024]{2,1,0:T(8,128)(2,1)S(1)}, u32[]{:S(2)}, u32[]{:S(2)}) async-start(bf16[64,8,1024]{2,1,0:T(8,128)(2,1)} %bitcast.27), calls=%async_computation.2 | async-start | bytes 2097152 | tf_op jit(solution)/shard_map/all_to_all | solution.py:606
  174.0 6.0 %copy-start.5 = (bf16[512,1536]{1,0:T(8,128)(2,1)S(1)}, bf16[512,1536]{1,0:T(8,128)(2,1)}, u32[]{:S(2)}) copy-start(bf16[512,1536]{1,0:T(8,128)(2,1)} %w_qkv.3) | copy-start | bytes 4718596
  174.0 6.0 %copy-start.14 = (f32[216,2048]{1,0:T(8,128)S(1)}, f32[216,2048]{1,0:T(8,128)}, u32[]{:S(2)}) copy-start(f32[216,2048]{1,0:T(8,128)} %get-tuple-element.76.grad_skip) | copy-start | bytes 5308420
  174.1 5.9 %copy-start.21 = (bf16[864,512]{1,0:T(8,128)(2,1)S(1)}, bf16[864,512]{1,0:T(8,128)(2,1)}, u32[]{:S(2)}) copy-start(bf16[864,512]{1,0:T(8,128)(2,1)} %copy-done.19) | copy-start | bytes 2654212
  174.1 5.9 %copy-start.23 = (f32[864,1]{1,0:T(8,128)S(1)}, f32[864,1]{1,0:T(8,128)}, u32[]{:S(2)}) copy-start(f32[864,1]{1,0:T(8,128)} %copy-done.22) | copy-start | bytes 10372
  177.7 9.9 %collective-permute-start.12 = (f32[16,512]{1,0:T(8,128)S(1)}, f32[16,512]{1,0:T(8,128)S(1)}, u32[]{:S(2)}, u32[]{:S(2)}) collective-permute-start(f32[16,512]{1,0:T(8,128)S(1)} %get-tuple-element.111), channel_id=1, source_target_pairs={{0,1},{1,0},{2,3},{3,2},{4,5},{5,4},{6,7},{7,6},{8,9},{9,8},{10,11... | collective-permute-start | bytes 98312 | tf_op jit(solution)/shard_map/ppermute | solution.py:48
  180.0 4.8 %copy-start.2 = (f32[216,2048]{1,0:T(8,128)S(1)}, f32[216,2048]{1,0:T(8,128)}, u32[]{:S(2)}) copy-start(f32[216,2048]{1,0:T(8,128)} %get-tuple-element.54.skip) | copy-start | bytes 5308420
  189.4 5.7 %collective-permute-start.11 = (f32[4,1024]{1,0:T(4,128)S(1)}, f32[4,1024]{1,0:T(4,128)S(1)}, u32[]{:S(2)}, u32[]{:S(2)}) collective-permute-start(f32[4,1024]{1,0:T(4,128)S(1)} %constant_dynamic-slice_fusion.2), channel_id=1, source_target_pairs={{0,1},{1,0},{2,3},{3,2},{4,5},{5,4},{6,7},{7,6},{8,9},{9,8},{10,11... | collective-permute-start | bytes 49160 | tf_op jit(solution)/shard_map/ppermute | solution.py:48

commit v3 on v2

--- a/solution.py
+++ b/solution.py
@@ -85,22 +85,19 @@
 
 
 def rims(fields, lat, before):
-    def cut(start, cols):
-        part = [field[:, start : start + cols] for field in fields]
-        close = [field.reshape(-1, field.shape[-1]) for field in part]
-        far = [lax.dynamic_slice_in_dim(field, (1 - lat) * SHIFT, SHIFT, 0) for field in part]
-        far = [field.reshape(-1, field.shape[-1]) for field in far]
-        return jnp.concatenate(close, axis=-1), jnp.concatenate(far, axis=-1)
-
     near = [lax.dynamic_slice_in_dim(field, (1 - lat) * SHIFT, SHIFT, 0) for field in fields]
     across = slide(jnp.concatenate(near, axis=-1), 1, 0)
     *fields, before = lax.optimization_barrier((*fields, before))
-    out = [across]
-    for step in (1, -1):
-        close, far = cut(COLS - SHIFT if step == 1 else 0, SHIFT)
-        out.append(slide(close, 0, step))
-        out.append(slide(far, 1, step))
-    return out, before
+
+    def cut(start):
+        parts = [field[:, start : start + SHIFT].reshape(-1, field.shape[-1]) for field in fields]
+        return jnp.concatenate(parts, axis=-1)
+
+    west, east = slide(cut(COLS - SHIFT), 0, 1), slide(cut(0), 0, -1)
+    count = SHIFT * SHIFT
+    passed = [lax.dynamic_slice_in_dim(side, (1 - lat) * count, count, 0) for side in (west, east)]
+    corners = slide(jnp.concatenate(passed, axis=0), 1, 0)
+    return [across, west, east, corners], before
 
 
 def dot(left, right):
@@ -111,10 +108,11 @@
     return lax.dot_general(left, right, (((1,), (1,)), ((), ())), preferred_element_type=F32)
 
 
-def lay_out(wide, own, across, west, west_far, east, east_far, groups, skipped=0):
+def lay_out(wide, own, across, west, east, corners, groups, skipped=0):
+    far = corners[...].astype(F32)
     sides = [
-        (0, west[...].astype(F32), west_far[...].astype(F32)),
-        (SHIFT + COLS, east[...].astype(F32), east_far[...].astype(F32)),
+        (0, west[...].astype(F32), far[: SHIFT * SHIFT]),
+        (SHIFT + COLS, east[...].astype(F32), far[SHIFT * SHIFT :]),
     ]
     for group in range(groups):
         lanes = slice(group * LANES, (group + 1) * LANES)
@@ -122,8 +120,8 @@
         for row in range(ROWS + SHIFT):
             centre = own[row, :, lanes] if row < ROWS else across[row - ROWS, :, rim_lanes]
             wide[group, row, SHIFT : SHIFT + COLS, :] = centre.astype(F32)
-            for start, close, far in sides:
-                part, at = (close, row) if row < ROWS else (far, row - ROWS)
+            for start, close, corner in sides:
+                part, at = (close, row) if row < ROWS else (corner, row - ROWS)
                 wide[group, row, start : start + SHIFT, :] = part[SHIFT * at : SHIFT * (at + 1), rim_lanes]
 
 
@@ -178,11 +176,11 @@
 
 
 def fine_forward_kernel(
-    spot, logit, own, across, west, west_far, east, east_far, table, w_qkv, w_out,
+    spot, logit, own, across, west, east, corners, table, w_qkv, w_out,
     skip, merged_norm, merged_spread, normed, spread, units, unit_scale, weights, attended,
     wide, embedded,
 ):
-    lay_out(wide, own, across, west, west_far, east, east_far, 5)
+    lay_out(wide, own, across, west, east, corners, 5)
     for win, pair, parity, row, cols in chunks(6):
         at = win * PATCHES + parity * CELLS + pair * 4
         for group in range(5):
@@ -258,8 +256,8 @@
         copies[chip] = block[...]
 
 
-def cotangent_kernel(own, across, west, west_far, east, east_far, merged, rounded, wide):
-    lay_out(wide, own, across, west, west_far, east, east_far, 4, D + LANES)
+def cotangent_kernel(own, across, west, east, corners, merged, rounded, wide):
+    lay_out(wide, own, across, west, east, corners, 4, D + LANES)
     for win, pair, parity, row, cols in chunks(6):
         at = win * CELLS + pair * 4
         for group in range(4):
@@ -270,13 +268,11 @@
 
 def coarse_kernel(
     norm, norm_other, cot, cot_other, parts,
-    coarse_out, grad_out, split, blocks,
-    merge, packed, coarse, grad_pre, sems,
+    coarse, grad_pre, split, blocks,
+    merge, packed, sems,
 ):
     load_merge = pltpu.make_async_copy(parts.at[:, :32], merge, sems.at[0])
     load_split = pltpu.make_async_copy(parts.at[:, 32:], packed, sems.at[1])
-    store_coarse = pltpu.make_async_copy(coarse, coarse_out, sems.at[2])
-    store_grad = pltpu.make_async_copy(grad_pre, grad_out, sems.at[3])
     load_split.start()
     load_merge.start()
     load_split.wait()
@@ -303,8 +299,6 @@
         grad_pre[i] = grad.astype(BF16)
         own_grads.append((grad * keep).astype(BF16))
         own_cots.append((coarse[i].astype(F32) * keep).astype(BF16))
-    store_coarse.start()
-    store_grad.start()
     for x in range(4):
         chips = slice(x * 16, (x + 1) * 16)
         lanes = slice(x * 512, (x + 1) * 512)
@@ -318,8 +312,6 @@
             quarters.append(block.reshape(64, 8, 512))
         pair = jnp.concatenate(quarters, axis=1).astype(BF16)
         blocks[:, 32 + 16 * j : 48 + 16 * j, :] = pair
-    store_coarse.wait()
-    store_grad.wait()
 
 
 def partial_kernel(
@@ -440,7 +432,7 @@
 
 
 def kernel_call(
-    kernel, name, outs, scratch, args, scalars=0, ahead=0, in_place=0, far_outs=0, flops=0, moved=0
+    kernel, name, outs, scratch, args, scalars=0, ahead=0, in_place=0, flops=0, moved=0
 ):
     count = len(args)
     specs = []
@@ -456,10 +448,7 @@
         kernel,
         out_shape=shapes,
         in_specs=specs,
-        out_specs=[
-            pl.BlockSpec(memory_space=pl.ANY if index < far_outs else pltpu.VMEM)
-            for index in range(len(outs))
-        ],
+        out_specs=[pl.BlockSpec(memory_space=pltpu.VMEM)] * len(outs),
         scratch_shapes=scratch,
         compiler_params=pltpu.CompilerParams(vmem_limit_bytes=VMEM_BYTES),
         cost_estimate=pl.CostEstimate(flops=flops, bytes_accessed=moved, transcendentals=0),
@@ -534,13 +523,10 @@
         [
             pltpu.VMEM((64, 32, 512), BF16),
             pltpu.VMEM((64, 32, 512), BF16),
-            pltpu.VMEM((2, ALL_CELLS, 512), BF16),
-            pltpu.VMEM((2, ALL_CELLS, 512), BF16),
-            pltpu.SemaphoreType.DMA((4,)),
+            pltpu.SemaphoreType.DMA((2,)),
         ],
         (merged_norm, norm_other, cot_rounded, cot_other, mine),
         in_place=1,
-        far_outs=2,
         flops=8_000_000_000,
         moved=15_000_000,
     )

time: 197 us -> 196 us (level)
    ppermute x5 -> x4, starting transfers between devices: 9.82 us -> 3.34 us  [slide(): return lax.ppermute(value, AXES, pairs)]
    ppermute x5 -> x4, waiting for transfers between devices: 5.14 us -> 10.3 us  [slide(): return lax.ppermute(value, AXES, pairs)]
    all_to_all x1, waiting for transfers between devices: 19.5 us -> 15.4 us  [per_device(): mine = lax.all_to_all(copies, CHIP_AXES, 0, 0, tiled=True)]
    ppermute x8, starting transfers between devices: 12.3 us -> 14.4 us  [move(): return lax.ppermute(value, AXES, pairs)]
  transfers between devices with their start and end apart: 16 -> 15, of which waited for: 7 -> 8; matrix products, arithmetic and copies ran while one was open for 5% -> 5% of each run, Pallas kernels for 31% -> 31%
where the time goes in v3:
time: 196 us; the launch traced here: 195 us
  Pallas kernels  71.2 us (36%)
  starting transfers between devices  56.5 us (29%)
  waiting for transfers between devices  42.5 us (22%)
  local copies, waits for them, and re-layouts  15.6 us (8%)
  other arithmetic  7.36 us (4%)
    pallas_call x8, Pallas kernels, kernel_call(): pl.pallas_call(kernel, out_shape=shapes, in_specs=specs, out_specs=[pl.Bl...  71.2 us
    all_to_all x1, starting transfers between devices, per_device(): blocks = lax.all_to_all(blocks, CHIP_AXES, 0, 0, tiled=True)  16 us
    all_to_all x1, waiting for transfers between devices, per_device(): mine = lax.all_to_all(copies, CHIP_AXES, 0, 0, tiled=True)  15.4 us
    ppermute x8, starting transfers between devices, move(): return lax.ppermute(value, AXES, pairs)  14.4 us
    all_to_all x1, starting transfers between devices, per_device(): mine = lax.all_to_all(copies, CHIP_AXES, 0, 0, tiled=True)  13.6 us
    unnamed x57, local copies, waits for them, and re-layouts  12.1 us
    ppermute x4, waiting for transfers between devices, slide(): return lax.ppermute(value, AXES, pairs)  10.3 us
    all_to_all x1, waiting for transfers between devices, per_device(): blocks = lax.all_to_all(blocks, CHIP_AXES, 0, 0, tiled=True)  9.67 us
  transfers between devices with their start and end apart: 15, of which 8 were waited for; matrix products, arithmetic and copies ran while one was open for 5% of the time, Pallas kernels for 31%

profile of v3, /device:TPU:1, one launch (start us, length us, event | category | flops | bytes accessed | tf_op | source)
XLA Modules:
  0.0 195.1 jit_solution(8680190648621553282)
XLA Ops:
  0.6 0.0 copy-start
  0.7 0.7 copy-done
  1.4 0.7 fusion.2
  2.2 1.5 collective-permute-start.1
  3.7 0.7 convert_element_type.23
  4.4 1.1 constant_dynamic-slice_fusion.5
  5.4 0.1 broadcast_in_dim.5
  5.5 0.1 pad_maximum_fusion.1
  5.6 1.4 collective-permute-start
  7.0 0.1 broadcast_in_dim.4
  7.1 0.1 fusion.25
  7.3 0.4 collective-permute-start.3
  7.7 1.5 collective-permute-start.2
  9.2 2.2 %collective-permute-done.3.east = bf16[32,1152]{1,0:T(8,128)(2,1)S(1)} collective-permute-done((bf16[32,1152]{1,0:T(8,128)(2,1)S(1)}, bf16[32,1152]{1,0:T(8,128)(2,1)S(1)}, u32[]{:S(2)}, u32[]{:S(2)}) %collective-permute-start.3) | collective-permute-done | bytes 73760 | tf_op jit(solution)/shard_map/ppermute | solution.py:56
  11.4 5.6 %collective-permute-done.2.west = bf16[32,1152]{1,0:T(8,128)(2,1)S(1)} collective-permute-done((bf16[32,1152]{1,0:T(8,128)(2,1)S(1)}, bf16[32,1152]{1,0:T(8,128)(2,1)S(1)}, u32[]{:S(2)}, u32[]{:S(2)}) %collective-permute-start.2) | collective-permute-done | bytes 73760 | tf_op jit(solution)/shard_map/ppermute | solution.py:56
  17.0 0.1 collective-permute-start.4
  17.1 0.3 spread_weights.1
  17.4 2.0 %copy-done.1 = bf16[64,64,512]{2,1,0:T(8,128)(2,1)} copy-done((bf16[64,64,512]{2,1,0:T(8,128)(2,1)}, bf16[64,64,512]{2,1,0:T(8,128)(2,1)S(1)}, u32[]{:S(2)}) %copy-start.1) | copy-done | bytes 4194328
  19.4 2.5 %collective-permute-done.4.corners = bf16[32,1152]{1,0:T(8,128)(2,1)S(1)} collective-permute-done((bf16[32,1152]{1,0:T(8,128)(2,1)S(1)}, bf16[32,1152]{1,0:T(8,128)(2,1)S(1)}, u32[]{:S(2)}, u32[]{:S(2)}) %collective-permute-start.4) | collective-permute-done | bytes 73760 | tf_op jit(solution)/shard_map/ppermute | solution.py:56
  21.9 13.6 %all-to-all-start = ((bf16[64,64,512]{2,1,0:T(8,128)(2,1)}), bf16[64,64,512]{2,1,0:T(8,128)(2,1)}, u32[]{:S(2)}, u32[]{:S(2)}) async-start(bf16[64,64,512]{2,1,0:T(8,128)(2,1)} %copy-done.1), calls=%async_computation | async-start | bytes 8388608 | tf_op jit(solution)/shard_map/all_to_all | solution.py:481
  35.6 0.1 pad_add_fusion.spot
  35.7 0.1 pad_maximum_fusion.own
  35.7 0.6 cotangent_cells.1
  36.4 1.2 copy-done.4
  37.6 5.4 %collective-permute-start.6 = (bf16[216,2048]{1,0:T(8,128)(2,1)S(1)}, bf16[216,2048]{1,0:T(8,128)(2,1)}, u32[]{:S(2)}, u32[]{:S(2)}) collective-permute-start(bf16[216,2048]{1,0:T(8,128)(2,1)S(1)} %get-tuple-element.57.cot), channel_id=1, source_target_pairs={{0,1},{1,0},{2,3},{3,2},{4,5},{5,4},{6,7},{7,6},{8,9},{9,8},{10,11... | collective-permute-start | bytes 2654216 | tf_op jit(solution)/shard_map/ppermute | solution.py:48
  43.0 22.3 %fine_forward.1 = (f32[216,2048]{1,0:T(8,128)}, bf16[216,2048]{1,0:T(8,128)(2,1)S(1)}, f32[216,1]{1,0:T(8,128)S(1)}, bf16[864,512]{1,0:T(8,128)(2,1)S(1)}, f32[8...) custom-call(s32[2]{0:T(128)S(1)} %pad_add_fusion.spot, ...), custom_call_target="tpu_custom_call" | custom-call | flops 15000000512 | bytes 12000000 | tf_op jit(solution)/shard_map/fine_forward/pallas_call | solution.py:447
  65.3 0.9 copy-done.19
  66.3 0.8 copy-done.22
  67.0 0.9 copy-done.24
  68.0 15.4 %all-to-all-done.parts = bf16[64,64,512]{2,1,0:T(8,128)(2,1)} async-done(((bf16[64,64,512]{2,1,0:T(8,128)(2,1)}), bf16[64,64,512]{2,1,0:T(8,128)(2,1)}, u32[]{:S(2)}, u32[]{:S(2)}) %all-to-all-start) | async-done | bytes 4194336 | tf_op jit(solution)/shard_map/all_to_all | solution.py:481
  83.4 10.6 %coarse.1 = (bf16[2,216,512]{2,1,0:T(8,128)(2,1)S(1)}, bf16[2,216,512]{2,1,0:T(8,128)(2,1)S(1)}, bf16[512,2048]{1,0:T(8,128)(2,1)}, bf16[64,64,512]{2,1,0:T(8,128)(2,1)}) custom-call(bf16[216,2048]{1,0:T(8,128)(2,1)S(1)} %get-tuple-element.56.norm.merged_norm, bf16[216,2048]{1,0:T(8,128)(2,1)S(1)} %collective-permute-done.5.norm_other, ...), custom_call_target="tpu_custom_call" | custom-call | flops 8000000000 | bytes 15000000 | tf_op jit(solution)/shard_map/coarse/pallas_call | solution.py:447
  94.0 0.8 copy-done.15
  94.8 0.8 copy-done.17
  95.5 16.0 %all-to-all-start.1 = ((bf16[64,64,512]{2,1,0:T(8,128)(2,1)}), bf16[64,64,512]{2,1,0:T(8,128)(2,1)}, u32[]{:S(2)}, u32[]{:S(2)}) async-start(bf16[64,64,512]{2,1,0:T(8,128)(2,1)} %get-tuple-element.79), calls=%async_computation.1 | async-start | bytes 8388608 | tf_op jit(solution)/shard_map/all_to_all | solution.py:534
  111.6 1.0 copy-done.18
  112.6 4.7 %partial_products.1 = (f32[216,2048]{1,0:T(8,128)S(1)}, bf16[216,2048]{1,0:T(8,128)(2,1)S(1)}, f32[216,2048]{1,0:T(8,128)S(1)}, bf16[216,2048]{1,0:T(8,128)(2,1)S(1)}) custom-call(bf16[64,64,512]{2,1,0:T(8,128)(2,1)} %all-to-all-done.parts, bf16[2,216,512]{2,1,0:T(8,128)(2,1)S(1)} %copy-done.16, bf16[2,216,512]{2,1,0:T(8,128)(2,1)S(1)} %copy-done.18, ...), custom_call_target="tpu_custom_call" | custom-call | flops 3000000000 | bytes 10000000 | tf_op jit(solution)/shard_map/partial_products/pallas_call | solution.py:447
  117.3 1.0 copy-done.6
  118.3 1.2 copy-done.13
  119.5 1.3 collective-permute-start.8
  120.8 2.1 %collective-permute-done.8.received = bf16[216,2048]{1,0:T(8,128)(2,1)S(1)} collective-permute-done((bf16[216,2048]{1,0:T(8,128)(2,1)S(1)}, bf16[216,2048]{1,0:T(8,128)(2,1)S(1)}, u32[]{:S(2)}, u32[]{:S(2)}) %collective-permute-start.8) | collective-permute-done | bytes 884768 | tf_op jit(solution)/shard_map/ppermute | solution.py:48
  122.9 25.4 %fine_backward.1 = (f32[216,2048]{1,0:T(8,128)}, bf16[864,1536]{1,0:T(8,128)(2,1)}, bf16[512,1024]{1,0:T(8,128)(2,1)S(1)}, bf16[512,1024]{1,0:T(8,128)(2,1)}) custom-call(s32[2]{0:T(128)S(1)} %pad_add_fusion.spot, f32[8]{0:T(128)S(1)} %copy-done.12, f32[216,2048]{1,0:T(8,128)} %copy-done.13, bf16[216,2048]{1,0:T(8,128)(2,1)S(1)} %collective-permute-done.8.received, ...), custom_call_target="tpu_custom_call" | custom-call | flops 15000000512 | bytes 15000000 | tf_op jit(solution)/shard_map/fine_backward/pallas_call | solution.py:447
  148.3 0.4 collective-permute-start.9
  148.7 0.1 collective-permute-start.7
  148.8 2.5 %collective-permute-done.9 = bf16[512,1024]{1,0:T(8,128)(2,1)} collective-permute-done((bf16[512,1024]{1,0:T(8,128)(2,1)}, bf16[512,1024]{1,0:T(8,128)(2,1)}, u32[]{:S(2)}, u32[]{:S(2)}) %collective-permute-start.9) | collective-permute-done | bytes 1048608 | tf_op jit(solution)/shard_map/ppermute | solution.py:48
  151.3 2.6 %add_convert_fusion = bf16[512,1024]{1,0:T(8,128)(2,1)} fusion(bf16[512,1024]{1,0:T(8,128)(2,1)} %collective-permute-done.9, bf16[512,1024]{1,0:T(8,128)(2,1)S(1)} %get-tuple-element.77), kind=kLoop, calls=%fused_computation.4 | loop fusion | flops 2097152 | bytes 3145728 | tf_op jit(solution)/shard_map/convert_element_type | solution.py:590
  153.9 9.7 %all-to-all-done.1 = bf16[64,64,512]{2,1,0:T(8,128)(2,1)} async-done(((bf16[64,64,512]{2,1,0:T(8,128)(2,1)}), bf16[64,64,512]{2,1,0:T(8,128)(2,1)}, u32[]{:S(2)}, u32[]{:S(2)}) %all-to-all-start.1) | async-done | bytes 4194336 | tf_op jit(solution)/shard_map/all_to_all | solution.py:534
  163.6 9.2 %all-to-all-start.2 = ((bf16[64,8,1024]{2,1,0:T(8,128)(2,1)}), bf16[64,8,1024]{2,1,0:T(8,128)(2,1)S(1)}, u32[]{:S(2)}, u32[]{:S(2)}) async-start(bf16[64,8,1024]{2,1,0:T(8,128)(2,1)} %bitcast.25), calls=%async_computation.2 | async-start | bytes 2097152 | tf_op jit(solution)/shard_map/all_to_all | solution.py:592
  172.8 3.0 %convert_reduce_fusion = f32[64,512]{1,0:T(8,128)S(1)} fusion(bf16[64,64,512]{2,1,0:T(8,128)(2,1)} %all-to-all-done.1), kind=kLoop, calls=%fused_computation | loop fusion | flops 4161536 | bytes 4325376 | tf_op jit(solution)/shard_map/reduce_sum | solution.py:73
  175.8 0.6 fusion.27
  176.5 1.8 collective-permute-start.11
  178.3 4.7 %field_grad.1 = bf16[8,64,512]{2,1,0:T(8,128)(2,1)} custom-call(f32[216,2048]{1,0:T(8,128)S(1)} %copy-done.14, bf16[864,1536]{1,0:T(8,128)(2,1)} %get-tuple-element.75.grad_packed, bf16[864,512]{1,0:T(8,128)(2,1)S(1)} %copy-done.21, f32[864,1]{1,0:T(8,128)S(1)} %copy-done.23, bf16[512,1536]{1,0:T(8,128)(2,1)S(1)} %copy-done.5), custom_call_target="tpu_custom_call" | custom-call | flops 4000000000 | bytes 8000000 | tf_op jit(solution)/shard_map/field_grad/pallas_call | solution.py:447
  183.0 2.5 %decode.1 = bf16[8,64,512]{2,1,0:T(8,128)(2,1)} custom-call(f32[216,2048]{1,0:T(8,128)S(1)} %copy-done.2, f32[216,2048]{1,0:T(8,128)S(1)} %get-tuple-element.63.out_mine, bf16[216,2048]{1,0:T(8,128)(2,1)} %collective-permute-done.7.received), custom_call_target="tpu_custom_call" | custom-call | bytes 8000000 | tf_op jit(solution)/shard_map/decode/pallas_call | solution.py:447
  185.6 0.1 copy.22
  185.7 0.1 copy.24
  185.9 0.0 collective-permute-done.11
  185.9 0.1 copy.23
  186.0 0.1 copy.25
  186.1 2.5 %all-to-all-done.2 = bf16[64,8,1024]{2,1,0:T(8,128)(2,1)S(1)} async-done(((bf16[64,8,1024]{2,1,0:T(8,128)(2,1)}), bf16[64,8,1024]{2,1,0:T(8,128)(2,1)S(1)}, u32[]{:S(2)}, u32[]{:S(2)}) %all-to-all-start.2) | async-done | bytes 1048608 | tf_op jit(solution)/shard_map/all_to_all | solution.py:592
  188.7 0.2 convert_reduce_fusion.1
  188.9 3.9 %collective-permute-start.10 = (f32[4,1024]{1,0:T(4,128)S(1)}, f32[4,1024]{1,0:T(4,128)S(1)}, u32[]{:S(2)}, u32[]{:S(2)}) collective-permute-start(f32[4,1024]{1,0:T(4,128)S(1)} %constant_dynamic-slice_fusion.2), channel_id=1, source_target_pairs={{0,1},{1,0},{2,3},{3,2},{4,5},{5,4},{6,7},{7,6},{8,9},{9,8},{10,11... | collective-permute-start | bytes 49160 | tf_op jit(solution)/shard_map/ppermute | solution.py:48
  192.7 0.3 copy.28
  193.0 0.8 copy.29
  193.8 0.6 fusion.29
  194.5 0.6 pad_maximum_fusion.6
  (70 shorter events, 0.3 us)
Async XLA Ops:
  0.6 0.8 copy-start
  0.6 6.5 %copy-start.3 = (bf16[8,64,512]{2,1,0:T(8,128)(2,1)S(1)}, bf16[8,64,512]{2,1,0:T(8,128)(2,1)}, u32[]{:S(2)}) copy-start(bf16[8,64,512]{2,1,0:T(8,128)(2,1)} %own.1) | copy-start | bytes 1572868
  0.7 6.5 %copy-start.26 = (bf16[8,64,512]{2,1,0:T(8,128)(2,1)S(1)}, bf16[8,64,512]{2,1,0:T(8,128)(2,1)}, u32[]{:S(2)}) copy-start(bf16[8,64,512]{2,1,0:T(8,128)(2,1)} %param.9) | copy-start | bytes 1572868
  2.1 15.0 %copy-start.27 = (bf16[8,2048]{1,0:T(8,128)(2,1)S(1)}, bf16[8,2048]{1,0:T(8,128)(2,1)}, u32[]{:S(2)}) copy-start(bf16[8,2048]{1,0:T(8,128)(2,1)} %param.16) | copy-start | bytes 98308
  2.2 4.8 %collective-permute-start.1 = (bf16[16,512]{1,0:T(8,128)(2,1)S(1)}, bf16[16,512]{1,0:T(8,128)(2,1)S(1)}, u32[]{:S(2)}, u32[]{:S(2)}) collective-permute-start(bf16[16,512]{1,0:T(8,128)(2,1)S(1)} %get-tuple-element.113), channel_id=1, source_target_pairs={{0,1},{1,0},{2,3},{3,2},{4,5},{5,4},{6,7},{7,6},{8,9},{9,8},{10,11... | collective-permute-start | bytes 49160 | tf_op jit(solution)/shard_map/ppermute | solution.py:48
  5.6 16.3 %collective-permute-start = (bf16[4,64,1152]{2,1,0:T(8,128)(2,1)S(1)}, bf16[4,64,1152]{2,1,0:T(8,128)(2,1)S(1)}, u32[]{:S(2)}, u32[]{:S(2)}) collective-permute-start(bf16[4,64,1152]{2,1,0:T(8,128)(2,1)S(1)} %pad_maximum_fusion.1), channel_id=1, source_target_pairs={{0,64},{1,65},{2,66},{3,67},{4,68},{5,69},{6,70},{7,71},{8,72},{9,... | collective-permute-start | bytes 1769480 | tf_op jit(solution)/shard_map/ppermute | solution.py:56
  7.3 4.1 %collective-permute-start.3 = (bf16[32,1152]{1,0:T(8,128)(2,1)S(1)}, bf16[32,1152]{1,0:T(8,128)(2,1)S(1)}, u32[]{:S(2)}, u32[]{:S(2)}) collective-permute-start(bf16[32,1152]{1,0:T(8,128)(2,1)S(1)} %pad_maximum_fusion.3), channel_id=1, source_target_pairs={{0,63},{1,0},{2,1},{3,2},{4,3},{5,4},{6,5},{7,6},{8,7},{9,8},{10,9... | collective-permute-start | bytes 221192 | tf_op jit(solution)/shard_map/ppermute | solution.py:56
  7.7 9.3 %collective-permute-start.2 = (bf16[32,1152]{1,0:T(8,128)(2,1)S(1)}, bf16[32,1152]{1,0:T(8,128)(2,1)S(1)}, u32[]{:S(2)}, u32[]{:S(2)}) collective-permute-start(bf16[32,1152]{1,0:T(8,128)(2,1)S(1)} %pad_maximum_fusion.2), channel_id=1, source_target_pairs={{0,1},{1,2},{2,3},{3,4},{4,5},{5,6},{6,7},{7,8},{8,9},{9,10},{10,1... | collective-permute-start | bytes 221192 | tf_op jit(solution)/shard_map/ppermute | solution.py:56
  17.0 4.9 %collective-permute-start.4 = (bf16[32,1152]{1,0:T(8,128)(2,1)S(1)}, bf16[32,1152]{1,0:T(8,128)(2,1)S(1)}, u32[]{:S(2)}, u32[]{:S(2)}) collective-permute-start(bf16[32,1152]{1,0:T(8,128)(2,1)S(1)} %pad_maximum_fusion.4), channel_id=1, source_target_pairs={{0,64},{1,65},{2,66},{3,67},{4,68},{5,69},{6,70},{7,71},{8,72},{9,... | collective-permute-start | bytes 221192 | tf_op jit(solution)/shard_map/ppermute | solution.py:56
  17.4 2.0 %copy-start.1 = (bf16[64,64,512]{2,1,0:T(8,128)(2,1)}, bf16[64,64,512]{2,1,0:T(8,128)(2,1)S(1)}, u32[]{:S(2)}) copy-start(bf16[64,64,512]{2,1,0:T(8,128)(2,1)S(1)} %spread_weights.1) | copy-start | bytes 12582916
  21.9 61.5 %all-to-all-start = ((bf16[64,64,512]{2,1,0:T(8,128)(2,1)}), bf16[64,64,512]{2,1,0:T(8,128)(2,1)}, u32[]{:S(2)}, u32[]{:S(2)}) async-start(bf16[64,64,512]{2,1,0:T(8,128)(2,1)} %copy-done.1), calls=%async_computation | async-start | bytes 8388608 | tf_op jit(solution)/shard_map/all_to_all | solution.py:481
  35.5 7.5 %copy-start.9 = (bf16[512,512]{1,0:T(8,128)(2,1)S(1)}, bf16[512,512]{1,0:T(8,128)(2,1)}, u32[]{:S(2)}) copy-start(bf16[512,512]{1,0:T(8,128)(2,1)} %w_out.3) | copy-start | bytes 1572868
  35.6 7.4 %copy-start.11 = (f32[3,512]{1,0:T(4,128)S(1)}, f32[3,512]{1,0:T(4,128)}, u32[]{:S(2)}) copy-start(f32[3,512]{1,0:T(4,128)} %table.1) | copy-start | bytes 18436
  35.6 7.4 %copy-start.12 = (f32[8]{0:T(128)S(1)}, f32[8]{0:T(128)}, u32[]{:S(2)}) copy-start(f32[8]{0:T(128)} %logit.3) | copy-start | bytes 100
  36.4 1.2 copy-start.4
  37.6 45.8 %collective-permute-start.6 = (bf16[216,2048]{1,0:T(8,128)(2,1)S(1)}, bf16[216,2048]{1,0:T(8,128)(2,1)}, u32[]{:S(2)}, u32[]{:S(2)}) collective-permute-start(bf16[216,2048]{1,0:T(8,128)(2,1)S(1)} %get-tuple-element.57.cot), channel_id=1, source_target_pairs={{0,1},{1,0},{2,3},{3,2},{4,5},{5,4},{6,7},{7,6},{8,9},{9,8},{10,11... | collective-permute-start | bytes 2654216 | tf_op jit(solution)/shard_map/ppermute | solution.py:48
  65.3 0.9 copy-start.19
  66.2 0.8 copy-start.22
  67.0 0.9 copy-start.24
  68.0 26.0 %copy-start.7 = (bf16[216,2048]{1,0:T(8,128)(2,1)}, bf16[216,2048]{1,0:T(8,128)(2,1)S(1)}, u32[]{:S(2)}) copy-start(bf16[216,2048]{1,0:T(8,128)(2,1)S(1)} %get-tuple-element.56.norm.merged_norm) | copy-start | bytes 2654212
  68.0 15.4 %collective-permute-start.5 = (bf16[216,2048]{1,0:T(8,128)(2,1)S(1)}, bf16[216,2048]{1,0:T(8,128)(2,1)S(1)}, u32[]{:S(2)}, u32[]{:S(2)}) collective-permute-start(bf16[216,2048]{1,0:T(8,128)(2,1)S(1)} %get-tuple-element.56.norm.merged_norm), channel_id=1, source_target_pairs={{0,1},{1,0},{2,3},{3,2},{4,5},{5,4},{6,7},{7,6},{8,9},{9,8},{10,11... | collective-permute-start | bytes 2654216 | tf_op jit(solution)/shard_map/ppermute | solution.py:48
  94.0 0.8 copy-start.15
  94.8 0.8 copy-start.17
  94.8 16.8 %copy-start.16 = (bf16[2,216,512]{2,1,0:T(8,128)(2,1)S(1)}, bf16[2,216,512]{2,1,0:T(8,128)(2,1)}, u32[]{:S(2)}) copy-start(bf16[2,216,512]{2,1,0:T(8,128)(2,1)} %copy-done.15) | copy-start | bytes 1327108
  95.5 68.1 %all-to-all-start.1 = ((bf16[64,64,512]{2,1,0:T(8,128)(2,1)}), bf16[64,64,512]{2,1,0:T(8,128)(2,1)}, u32[]{:S(2)}, u32[]{:S(2)}) async-start(bf16[64,64,512]{2,1,0:T(8,128)(2,1)} %get-tuple-element.79), calls=%async_computation.1 | async-start | bytes 8388608 | tf_op jit(solution)/shard_map/all_to_all | solution.py:534
  111.6 1.0 copy-start.18
  112.6 10.3 %copy-start.8 = (bf16[216,2048]{1,0:T(8,128)(2,1)S(1)}, bf16[216,2048]{1,0:T(8,128)(2,1)}, u32[]{:S(2)}) copy-start(bf16[216,2048]{1,0:T(8,128)(2,1)} %copy-done.7) | copy-start | bytes 2654212
  112.6 10.3 %copy-start.10 = (bf16[512,512]{1,0:T(8,128)(2,1)S(1)}, bf16[512,512]{1,0:T(8,128)(2,1)}, u32[]{:S(2)}) copy-start(bf16[512,512]{1,0:T(8,128)(2,1)} %w_out.3) | copy-start | bytes 1572868
  112.6 10.3 %copy-start.20 = (bf16[864,512]{1,0:T(8,128)(2,1)S(1)}, bf16[864,512]{1,0:T(8,128)(2,1)}, u32[]{:S(2)}) copy-start(bf16[864,512]{1,0:T(8,128)(2,1)} %copy-done.19) | copy-start | bytes 2654212
  112.6 10.3 %copy-start.25 = (bf16[864,512]{1,0:T(8,128)(2,1)S(1)}, bf16[864,512]{1,0:T(8,128)(2,1)}, u32[]{:S(2)}) copy-start(bf16[864,512]{1,0:T(8,128)(2,1)} %copy-done.24) | copy-start | bytes 2654212
  117.3 1.0 copy-start.6
  118.3 1.2 copy-start.13
  119.5 3.4 %collective-permute-start.8 = (bf16[216,2048]{1,0:T(8,128)(2,1)S(1)}, bf16[216,2048]{1,0:T(8,128)(2,1)S(1)}, u32[]{:S(2)}, u32[]{:S(2)}) collective-permute-start(bf16[216,2048]{1,0:T(8,128)(2,1)S(1)} %get-tuple-element.66), channel_id=1, source_target_pairs={{0,1},{1,0},{2,3},{3,2},{4,5},{5,4},{6,7},{7,6},{8,9},{9,8},{10,11... | collective-permute-start | bytes 2654216 | tf_op jit(solution)/shard_map/ppermute | solution.py:48
  148.3 3.0 %collective-permute-start.9 = (bf16[512,1024]{1,0:T(8,128)(2,1)}, bf16[512,1024]{1,0:T(8,128)(2,1)}, u32[]{:S(2)}, u32[]{:S(2)}) collective-permute-start(bf16[512,1024]{1,0:T(8,128)(2,1)} %get-tuple-element.78), channel_id=1, source_target_pairs={{0,1},{1,0},{2,3},{3,2},{4,5},{5,4},{6,7},{7,6},{8,9},{9,8},{10,11... | collective-permute-start | bytes 3145736 | tf_op jit(solution)/shard_map/ppermute | solution.py:48
  148.7 34.3 %collective-permute-start.7 = (bf16[216,2048]{1,0:T(8,128)(2,1)}, bf16[216,2048]{1,0:T(8,128)(2,1)}, u32[]{:S(2)}, u32[]{:S(2)}) collective-permute-start(bf16[216,2048]{1,0:T(8,128)(2,1)} %copy-done.6), channel_id=1, source_target_pairs={{0,1},{1,0},{2,3},{3,2},{4,5},{5,4},{6,7},{7,6},{8,9},{9,8},{10,11... | collective-permute-start | bytes 2654216 | tf_op jit(solution)/shard_map/ppermute | solution.py:48
  163.6 25.1 %all-to-all-start.2 = ((bf16[64,8,1024]{2,1,0:T(8,128)(2,1)}), bf16[64,8,1024]{2,1,0:T(8,128)(2,1)S(1)}, u32[]{:S(2)}, u32[]{:S(2)}) async-start(bf16[64,8,1024]{2,1,0:T(8,128)(2,1)} %bitcast.25), calls=%async_computation.2 | async-start | bytes 2097152 | tf_op jit(solution)/shard_map/all_to_all | solution.py:592
  172.8 5.5 %copy-start.5 = (bf16[512,1536]{1,0:T(8,128)(2,1)S(1)}, bf16[512,1536]{1,0:T(8,128)(2,1)}, u32[]{:S(2)}) copy-start(bf16[512,1536]{1,0:T(8,128)(2,1)} %w_qkv.3) | copy-start | bytes 4718596
  172.8 5.5 %copy-start.14 = (f32[216,2048]{1,0:T(8,128)S(1)}, f32[216,2048]{1,0:T(8,128)}, u32[]{:S(2)}) copy-start(f32[216,2048]{1,0:T(8,128)} %get-tuple-element.74.grad_skip) | copy-start | bytes 5308420
  172.8 5.5 %copy-start.21 = (bf16[864,512]{1,0:T(8,128)(2,1)S(1)}, bf16[864,512]{1,0:T(8,128)(2,1)}, u32[]{:S(2)}) copy-start(bf16[864,512]{1,0:T(8,128)(2,1)} %copy-done.19) | copy-start | bytes 2654212
  172.8 5.5 %copy-start.23 = (f32[864,1]{1,0:T(8,128)S(1)}, f32[864,1]{1,0:T(8,128)}, u32[]{:S(2)}) copy-start(f32[864,1]{1,0:T(8,128)} %copy-done.22) | copy-start | bytes 10372
  176.5 9.4 %collective-permute-start.11 = (f32[16,512]{1,0:T(8,128)S(1)}, f32[16,512]{1,0:T(8,128)S(1)}, u32[]{:S(2)}, u32[]{:S(2)}) collective-permute-start(f32[16,512]{1,0:T(8,128)S(1)} %get-tuple-element.109), channel_id=1, source_target_pairs={{0,1},{1,0},{2,3},{3,2},{4,5},{5,4},{6,7},{7,6},{8,9},{9,8},{10,11... | collective-permute-start | bytes 98312 | tf_op jit(solution)/shard_map/ppermute | solution.py:48
  178.3 4.8 %copy-start.2 = (f32[216,2048]{1,0:T(8,128)S(1)}, f32[216,2048]{1,0:T(8,128)}, u32[]{:S(2)}) copy-start(f32[216,2048]{1,0:T(8,128)} %get-tuple-element.52.skip) | copy-start | bytes 5308420
  188.9 5.0 %collective-permute-start.10 = (f32[4,1024]{1,0:T(4,128)S(1)}, f32[4,1024]{1,0:T(4,128)S(1)}, u32[]{:S(2)}, u32[]{:S(2)}) collective-permute-start(f32[4,1024]{1,0:T(4,128)S(1)} %constant_dynamic-slice_fusion.2), channel_id=1, source_target_pairs={{0,1},{1,0},{2,3},{3,2},{4,5},{5,4},{6,7},{7,6},{8,9},{9,8},{10,11... | collective-permute-start | bytes 49160 | tf_op jit(solution)/shard_map/ppermute | solution.py:48
